TPU v7x, 256 devices: a whole 4x4x8 slice. The times are simulated.
256 devices in a mesh: guide: 2 (over core), seq: 32 (over x, z), rep: 4 (over y).
Axes of the slice: x: 4, y: 4, z: 8, core: 2. Of those that a mesh axis runs over, the one named last changes fastest.
Arguments:
- queries: bfloat16 [2, 16384, 4096], P('guide', ('seq', 'rep')), may hold values from -12 to 12
- key_vectors: bfloat16 [2, 16384, 4096], P('guide', ('seq', 'rep')), may hold values from -12 to 12
- value_vectors: bfloat16 [2, 16384, 4096], P('guide', ('seq', 'rep')), may hold values from -6 to 6
- cluster_order: int32 [32, 16384], P('seq'), may hold values from 0 to 16383, as said below
- key_blocks: int32 [32, 64, 8], P('seq'), may hold values from 0 to 63, as said below
- extents: int32 [32, 64], P('seq'), may hold values from 1 to 8, as said below
Outputs:
- guided: bfloat16 [16384, 4096], P(('seq', 'rep'), 'guide')
Inputs may be any that keep to these rules, and one draw needn't show every extreme that they name: `cluster_order`: each row is a permutation of the 16384 tokens. Entry 0 of key_blocks[h, c] is c itself, and the entries of one row are distinct. Only the first extents[h, c] entries of key_blocks[h, c] are listed; the value 8 occurs in every draw.
All inputs are finite; a program needn't handle non-finite values.
Results may differ from a plain program's by a relative error of at most 0.0057.
Values may be sent and summed in bfloat16 or wider, within the bound.
A program may use at most 128 MiB of HBM per device.

v0:
```python
import jax
import jax.numpy as jnp
from jax import lax
from jax.sharding import PartitionSpec as P

CLUSTER = 256


GUIDE_SCALE = 5.0


def attend_padded(sorted_queries, sorted_keys, sorted_values, listed, counts):
    cluster_count, rows, head_dim = sorted_queries.shape
    blocks_most = listed.shape[1]
    group_size = 2

    def one_group(packed):
        group_queries, group_list, group_counts = packed
        block_keys = sorted_keys[group_list].reshape(group_size, blocks_most * rows, head_dim)
        block_values = sorted_values[group_list].reshape(group_size, blocks_most * rows, head_dim)
        scores = jnp.einsum(
            "gqd,gkd->gqk", group_queries, block_keys, preferred_element_type=jnp.float32
        ) * head_dim ** (-0.5)
        live_mask = jnp.repeat(
            jnp.arange(blocks_most)[None, :] < group_counts[:, None], rows, axis=1
        )
        scores = jnp.where(live_mask[:, None, :], scores, -jnp.inf)
        shifted = jnp.exp(scores - jnp.max(scores, axis=2, keepdims=True))
        weights = (shifted / jnp.sum(shifted, axis=2, keepdims=True)).astype(jnp.bfloat16)
        return jnp.einsum(
            "gqk,gkd->gqd", weights, block_values, preferred_element_type=jnp.float32
        ).astype(jnp.bfloat16)

    result = lax.map(
        one_group,
        (
            sorted_queries.reshape(cluster_count // group_size, group_size, rows, head_dim),
            listed.reshape(cluster_count // group_size, group_size, blocks_most),
            counts.reshape(cluster_count // group_size, group_size),
        ),
    )
    return result.reshape(cluster_count * rows, head_dim)


def on_device(queries, key_vectors, value_vectors, cluster_order, key_blocks, extents):
    seq_count = lax.axis_size("seq")
    rep_count = lax.axis_size("rep")
    local_queries = queries[0]
    local_keys = key_vectors[0]
    local_values = value_vectors[0]
    tok_dev = local_queries.shape[0]
    heads_local = cluster_order.shape[0]
    tokens = cluster_order.shape[1]
    head_dim = local_queries.shape[1] // (heads_local * seq_count)
    gathered = (
        lax.all_gather(local_queries, "rep", axis=0, tiled=True),
        lax.all_gather(local_keys, "rep", axis=0, tiled=True),
        lax.all_gather(local_values, "rep", axis=0, tiled=True),
    )
    all_queries, all_keys, all_values = (
        lax.all_to_all(gathered[0], "seq", split_axis=1, concat_axis=0, tiled=True),
        lax.all_to_all(gathered[1], "seq", split_axis=1, concat_axis=0, tiled=True),
        lax.all_to_all(gathered[2], "seq", split_axis=1, concat_axis=0, tiled=True),
    )
    query_span = tokens // rep_count
    own_clusters = query_span // CLUSTER
    rep_index = lax.axis_index("rep")
    first_row = rep_index * query_span
    rows_sorted = cluster_order[0]
    head_keys = jnp.take(all_keys, rows_sorted, axis=0)
    head_values = jnp.take(all_values, rows_sorted, axis=0)
    head_keys = head_keys.reshape(tokens // CLUSTER, CLUSTER, head_dim)
    head_values = head_values.reshape(tokens // CLUSTER, CLUSTER, head_dim)
    query_rows = lax.dynamic_slice_in_dim(rows_sorted, first_row, query_span)
    head_queries = jnp.take(all_queries, query_rows, axis=0)
    head_queries = head_queries.reshape(own_clusters, CLUSTER, head_dim)
    listed = lax.dynamic_slice_in_dim(key_blocks[0], rep_index * own_clusters, own_clusters)
    counts = lax.dynamic_slice_in_dim(extents[0], rep_index * own_clusters, own_clusters)
    attended = attend_padded(head_queries, head_keys, head_values, listed, counts)
    pieces = jnp.zeros((tokens, head_dim), jnp.bfloat16).at[query_rows].set(attended)
    parted = lax.all_to_all(pieces, "seq", split_axis=0, concat_axis=1, tiled=True)
    attention_out = lax.psum_scatter(
        parted.astype(jnp.float32).astype(jnp.bfloat16), "rep", scatter_dimension=0, tiled=True
    )
    paired = lax.all_to_all(attention_out, "guide", split_axis=1, concat_axis=0, tiled=True)
    conditioned = paired[:tok_dev].astype(jnp.float32)
    unconditioned = paired[tok_dev:].astype(jnp.float32)
    return (unconditioned + GUIDE_SCALE * (conditioned - unconditioned)).astype(jnp.bfloat16)


def solution(mesh):
    placed = (
        P("guide", ("seq", "rep"), None),
        P("guide", ("seq", "rep"), None),
        P("guide", ("seq", "rep"), None),
        P("seq", None),
        P("seq", None, None),
        P("seq", None),
    )
    return jax.shard_map(
        on_device, mesh=mesh, in_specs=placed, out_specs=P(("seq", "rep"), "guide"), check_vma=False
    )
```

profile of v0, /device:TPU:6, one launch (start us, length us, event | category | flops | bytes accessed | tf_op | source)
XLA Modules:
  0.0 699.9 jit_solution(13783845832581200339)
XLA Ops:
  6.5 0.7 all-gather.9.cloned.1.call-update
  7.3 55.7 %all-gather.9.cloned.1.call-done = bf16[1,512,4096]{2,1,0:T(8,128)(2,1)} async-done(((bf16[1,128,4096]{2,1,0:T(8,128)(2,1)}), bf16[1,512,4096]{2,1,0:T(8,128)(2,1)}) %all-gather.9.cloned.1.call-update) | async-done | bytes 4194320 | tf_op jit(solution)/shard_map/all_gather | solution.py:57
  63.0 3.4 copy.33
  66.4 3.6 copy.24
  70.0 10.2 %all-to-all-start.1 = ((bf16[512,32,128]{2,0,1:T(8,128)(2,1)}), bf16[512,32,128]{2,0,1:T(8,128)(2,1)}, u32[]{:S(2)}, u32[]{:S(2)}) async-start(bf16[512,32,128]{2,0,1:T(8,128)(2,1)} %copy.24), calls=%async_computation.1 | async-start | bytes 8388608 | tf_op jit(solution)/shard_map/all_to_all | solution.py:62
  80.3 0.7 all-gather.11.cloned.1.call-update
  81.0 52.7 %all-gather.11.cloned.1.call-done = bf16[1,512,4096]{2,1,0:T(8,128)(2,1)} async-done(((bf16[1,128,4096]{2,1,0:T(8,128)(2,1)}), bf16[1,512,4096]{2,1,0:T(8,128)(2,1)}) %all-gather.11.cloned.1.call-update) | async-done | bytes 4194320 | tf_op jit(solution)/shard_map/all_gather | solution.py:58
  133.7 3.4 copy.34
  137.1 3.6 copy.25
  140.7 32.9 %all-to-all-done.1 = bf16[512,32,128]{2,0,1:T(8,128)(2,1)} async-done(((bf16[512,32,128]{2,0,1:T(8,128)(2,1)}), bf16[512,32,128]{2,0,1:T(8,128)(2,1)}, u32[]{:S(2)}, u32[]{:S(2)}) %all-to-all-start.1) | async-done | bytes 4194336 | tf_op jit(solution)/shard_map/all_to_all | solution.py:62
  173.6 8.8 %all-to-all-start.2 = ((bf16[512,32,128]{2,0,1:T(8,128)(2,1)}), bf16[512,32,128]{2,0,1:T(8,128)(2,1)}, u32[]{:S(2)}, u32[]{:S(2)}) async-start(bf16[512,32,128]{2,0,1:T(8,128)(2,1)} %copy.25), calls=%async_computation.2 | async-start | bytes 8388608 | tf_op jit(solution)/shard_map/all_to_all | solution.py:63
  182.5 0.7 all-gather.7.cloned.1.call-update
  183.2 52.7 %all-gather.7.cloned.1.call-done = bf16[1,512,4096]{2,1,0:T(8,128)(2,1)} async-done(((bf16[1,128,4096]{2,1,0:T(8,128)(2,1)}), bf16[1,512,4096]{2,1,0:T(8,128)(2,1)}) %all-gather.7.cloned.1.call-update) | async-done | bytes 4194320 | tf_op jit(solution)/shard_map/all_gather | solution.py:56
  236.0 3.4 copy.32
  239.4 3.6 copy.22
  243.0 32.9 %all-to-all-done.2 = bf16[512,32,128]{2,0,1:T(8,128)(2,1)} async-done(((bf16[512,32,128]{2,0,1:T(8,128)(2,1)}), bf16[512,32,128]{2,0,1:T(8,128)(2,1)}, u32[]{:S(2)}, u32[]{:S(2)}) %all-to-all-start.2) | async-done | bytes 4194336 | tf_op jit(solution)/shard_map/all_to_all | solution.py:63
  275.9 9.0 %all-to-all-start = ((bf16[512,32,128]{2,0,1:T(8,128)(2,1)}), bf16[512,32,128]{2,0,1:T(8,128)(2,1)}, u32[]{:S(2)}, u32[]{:S(2)}) async-start(bf16[512,32,128]{2,0,1:T(8,128)(2,1)} %copy.22), calls=%async_computation | async-start | bytes 8388608 | tf_op jit(solution)/shard_map/all_to_all | solution.py:61
  284.9 0.2 reduce-scatter.4.cloned.1.call-start
  285.7 58.2 %gather_fusion.3 = bf16[16384,128]{1,0:T(8,128)(2,1)} fusion(bf16[16384,128]{1,0:T(8,128)(2,1)} %bitcast.14, s32[16384]{0:T(1024)S(1)} %fusion.41), kind=kCustom, calls=%fused_computation.clone | custom fusion | bytes 8454144 | tf_op jit(solution)/shard_map/jit(_take)/gather | solution.py:70
  343.9 58.2 %gather_fusion.4 = bf16[16384,128]{1,0:T(8,128)(2,1)} fusion(bf16[16384,128]{1,0:T(8,128)(2,1)} %bitcast.17, s32[16384]{0:T(1024)S(1)} %fusion.41), kind=kCustom, calls=%fused_computation.3.clone | custom fusion | bytes 8454144 | tf_op jit(solution)/shard_map/jit(_take)/gather | solution.py:71
  402.1 13.8 %gather_fusion.2 = bf16[4096,128]{1,0:T(8,128)(2,1)S(1)} fusion(bf16[16384,128]{1,0:T(8,128)(2,1)} %bitcast.9, s32[4096]{0:T(1024)S(1)} %broadcast_clamp_fusion), kind=kCustom, calls=%fused_computation.4 | custom fusion | bytes 2113536 | tf_op jit(solution)/shard_map/jit(_take)/gather | solution.py:75
  415.9 0.7 broadcast_select_fusion.2
  416.6 13.1 %broadcast_select_fusion = (bf16[16384,128]{1,0:T(8,128)(2,1)}, bf16[16384,128]{1,0:T(8,128)(2,1)}) fusion(bf16[16384,128]{1,0:T(8,128)(2,1)} %gather_fusion.4, pred[16384]{0:T(1024)(128)(4,1)S(1)} %compare_and_fusion, bf16[16384,128]{1,0:T(8,128)(2,1)} %gather_fusion.3), kind=kLoop, calls=%fused_computation.37 | loop fusion | flops 4194304 | bytes 16793600 | tf_op jit(solution)/shard_map/jit(_take)/select_n | solution.py:71
  429.7 79.5 %while.10 = (s32[]{:T(128)}, bf16[8,2,256,128]{3,2,1,0:T(8,128)(2,1)}, s32[8,2]{1,0:T(8,128)S(1)}, bf16[8,2,256,128]{3,2,1,0:T(8,128)(2,1)S(1)}, s32[8,2,8]{2,1,...) while((s32[]{:T(128)}, bf16[8,2,256,128]{3,2,1,0:T(8,128)(2,1)}, ...), condition=%wide.region_3.5_spmd, body=%wide.region_0.4_spmd.sunk | while | flops 814814784 | bytes 7771737 | solution.py:34
  429.8 2.9 gather_fusion.1
  432.9 1.4 fusion.63
  434.3 2.9 gather_fusion
  437.2 2.4 fusion.64
  439.7 2.9 gather_fusion.1
  442.8 1.4 fusion.63
  444.2 2.9 gather_fusion
  447.2 2.4 fusion.64
  449.6 2.9 gather_fusion.1
  452.8 1.4 fusion.63
  454.1 2.9 gather_fusion
  457.1 2.4 fusion.64
  459.6 2.9 gather_fusion.1
  462.7 1.4 fusion.63
  464.1 2.9 gather_fusion
  467.0 2.4 fusion.64
  469.5 2.9 gather_fusion.1
  472.6 1.4 fusion.63
  474.0 2.9 gather_fusion
  477.0 2.4 fusion.64
  479.4 2.9 gather_fusion.1
  482.5 1.4 fusion.63
  483.9 2.9 gather_fusion
  486.9 2.4 fusion.64
  489.4 2.9 gather_fusion.1
  492.5 1.4 fusion.63
  493.9 2.9 gather_fusion
  496.8 2.4 fusion.64
  499.3 2.9 gather_fusion.1
  502.4 1.4 fusion.63
  503.8 2.9 gather_fusion
  506.8 2.4 fusion.64
  509.2 13.8 %scatter_custom_fusion = bf16[16384,128]{1,0:T(8,128)(2,1)} fusion(s32[4096]{0:T(1024)S(1)} %bitcast.121, bf16[4096,128]{1,0:T(8,128)(2,1)} %bitcast.123, bf16[]{:T(256)} %constant.37.clone.1), kind=kCustom, calls=%fused_computation.39 | custom fusion | bytes 4194816 | tf_op jit(solution)/shard_map/scatter | solution.py:80
  523.0 103.1 %all_to_all.92 = bf16[32,512,128]{2,1,0:T(8,128)(2,1)} all-to-all(bf16[32,512,128]{2,1,0:T(8,128)(2,1)} %bitcast.104), channel_id=1, replica_groups=mesh['guide'=2,'seq'=32,'rep'=4] {'seq'}, dimensions={0} | all-to-all | bytes 8388608 | tf_op jit(solution)/shard_map/all_to_all | solution.py:81
  626.1 6.5 copy.26
  632.6 6.5 copy.28
  639.1 46.8 %reduce-scatter.4.cloned.1.call-done = bf16[128,4096]{1,0:T(8,128)(2,1)} async-done(((bf16[512,4096]{1,0:T(8,128)(2,1)}), bf16[128,4096]{1,0:T(8,128)(2,1)}) %reduce-scatter.4.cloned.1.call-update) | async-done | bytes 1048592
  685.9 1.6 copy.29
  687.5 4.6 all_to_all.93
  692.3 1.0 copy.27
  (82 shorter events, 3.0 us)
Async XLA Ops:
  6.5 278.7 %copy-start = (s32[1,64,8]{1,2,0:T(8,128)S(1)}, s32[1,64,8]{1,2,0:T(8,128)}, u32[]{:S(2)}) copy-start(s32[1,64,8]{1,2,0:T(8,128)} %param.14) | copy-start | bytes 6148
  6.5 56.4 %all-gather.9.cloned.1.call-start = ((), (), s32[]{:S(2)}) async-start(), calls=%async_computation.7 | async-start | bytes 5242880 | tf_op jit(solution)/shard_map/all_gather | solution.py:57
  70.0 103.6 %all-to-all-start.1 = ((bf16[512,32,128]{2,0,1:T(8,128)(2,1)}), bf16[512,32,128]{2,0,1:T(8,128)(2,1)}, u32[]{:S(2)}, u32[]{:S(2)}) async-start(bf16[512,32,128]{2,0,1:T(8,128)(2,1)} %copy.24), calls=%async_computation.1 | async-start | bytes 8388608 | tf_op jit(solution)/shard_map/all_to_all | solution.py:62
  80.2 53.5 %all-gather.11.cloned.1.call-start = ((), (), s32[]{:S(2)}) async-start(), calls=%async_computation.8 | async-start | bytes 5242880 | tf_op jit(solution)/shard_map/all_gather | solution.py:58
  173.6 102.2 %all-to-all-start.2 = ((bf16[512,32,128]{2,0,1:T(8,128)(2,1)}), bf16[512,32,128]{2,0,1:T(8,128)(2,1)}, u32[]{:S(2)}, u32[]{:S(2)}) async-start(bf16[512,32,128]{2,0,1:T(8,128)(2,1)} %copy.25), calls=%async_computation.2 | async-start | bytes 8388608 | tf_op jit(solution)/shard_map/all_to_all | solution.py:63
  182.5 53.5 %all-gather.7.cloned.1.call-start = ((), (), s32[]{:S(2)}) async-start(), calls=%async_computation.6 | async-start | bytes 5242880 | tf_op jit(solution)/shard_map/all_gather | solution.py:56
  243.0 42.2 %copy-start.2 = (s32[1,16384]{1,0:T(1,128)S(1)}, s32[1,16384]{1,0:T(1,128)}, u32[]{:S(2)}) copy-start(s32[1,16384]{1,0:T(1,128)} %param.13) | copy-start | bytes 196612
  243.0 42.4 %copy-start.3 = (s32[1,64]{1,0:T(1,128)S(1)}, s32[1,64]{1,0:T(1,128)}, u32[]{:S(2)}) copy-start(s32[1,64]{1,0:T(1,128)} %param.15) | copy-start | bytes 772
  275.9 126.2 %all-to-all-start = ((bf16[512,32,128]{2,0,1:T(8,128)(2,1)}), bf16[512,32,128]{2,0,1:T(8,128)(2,1)}, u32[]{:S(2)}, u32[]{:S(2)}) async-start(bf16[512,32,128]{2,0,1:T(8,128)(2,1)} %copy.22), calls=%async_computation | async-start | bytes 8388608 | tf_op jit(solution)/shard_map/all_to_all | solution.py:61
  284.9 401.0 %reduce-scatter.4.cloned.1.call-start = ((), (), s32[]{:S(2)}) async-start(), calls=%async_computation.9 | async-start | bytes 5242880
  639.1 54.2 %copy-start.1 = (s32[1,64,8]{1,2,0:T(8,128)S(1)}, s32[1,64,8]{1,2,0:T(8,128)}, u32[]{:S(2)}) copy-start(s32[1,64,8]{1,2,0:T(8,128)} %param.14) | copy-start | bytes 6148
Sparse Core Ops, SparseCore 0:
  9.2 53.7 all-gather.8
  82.9 50.7 all-gather.10
  185.1 50.7 all-gather.6
  639.2 46.6 reduce-scatter.3
where the time goes:
time: 703 us; the launch traced here: 700 us
  waiting for transfers between devices  276 us (39%)
  local copies, waits for them, and re-layouts  229 us (33%)
  blocking collectives  108 us (15%)
  matrix products  30.1 us (4%)
  starting transfers between devices  28.4 us (4%)
  other arithmetic  14.8 us (2%)
  between operations  13.3 us (2%)
    all_to_all x1, blocking collectives, on_device(): lax.all_to_all(pieces, 'seq', split_axis=0, concat_axis=1, tiled=True)  103 us
    gather x1, local copies, waits for them, and re-layouts, on_device(): head_keys = jnp.take(all_keys, rows_sorted, axis=0)  58.2 us
    gather x1, local copies, waits for them, and re-layouts, on_device(): head_values = jnp.take(all_values, rows_sorted, axis=0)  58.2 us
    all_gather x1, waiting for transfers between devices, on_device(): lax.all_gather(local_keys, 'rep', axis=0, tiled=True)  55.7 us
    all_gather x1, waiting for transfers between devices, on_device(): lax.all_gather(local_queries, 'rep', axis=0, tiled=True)  52.7 us
    all_gather x1, waiting for transfers between devices, on_device(): lax.all_gather(local_values, 'rep', axis=0, tiled=True)  52.7 us
    unnamed x5, waiting for transfers between devices  48.9 us
    all_to_all x1, waiting for transfers between devices, on_device(): lax.all_to_all(gathered[1], 'seq', split_axis=1, concat_axis=0, tiled=True)  32.9 us
  transfers between devices with their start and end apart: 7, of which 6 were waited for; matrix products, arithmetic and copies ran while one was open for 19% of the time, Pallas kernels for 0%

commit v1 on v0

v1 whole, which is shorter than its diff:
```python
import functools

import jax
import jax.numpy as jnp
from jax import lax
from jax.experimental import pallas as pl
from jax.experimental.pallas import tpu as pltpu
from jax.sharding import PartitionSpec as P

MESH = pl.DeviceIdType.MESH
CLUSTER = 256
GUIDE_SCALE = 5.0
HEADS = 32
SEQ_X, SEQ_Z = 4, 8
REPS = 4
TOKENS = 16384
DIM = 128
SPAN = TOKENS // REPS
LOCAL = 128
CLUSTERS = TOKENS // CLUSTER
CHUNK = 512
CHUNKS = SPAN // CHUNK
WINDOW = 128
QROWS = 96
f32, bf16, i32 = jnp.float32, jnp.bfloat16, jnp.int32

NT = (((1,), (1,)), ((), ()))


def dot_nt(a, b):
    return lax.dot_general(a, b, NT, preferred_element_type=f32)


def iota(shape, dim):
    return lax.broadcasted_iota(i32, shape, dim)


def gather_kernel(q_in, k_in, v_in, order_ref, kall, vall, qs, dest_out, destt_out,
                  rx, sorted_, onehot, key_s, low_s, rhi_s, rlo_s, dest_s, destt_s,
                  send_sem, recv_sem, own_sem, ysend, yrecv, out_sem):
    me = lax.axis_index("seq")
    rep = lax.axis_index("rep")
    x, z = me // SEQ_Z, me % SEQ_Z
    right, left = lax.rem(rep + 1, REPS), lax.rem(rep + REPS - 1, REPS)
    ins = (k_in, v_in, q_in)
    alls = (kall, vall)

    def peer_of(off):
        return lax.rem(x + off // SEQ_Z, SEQ_X) * SEQ_Z + lax.rem(z + off % SEQ_Z, SEQ_Z)

    barrier = pltpu.get_barrier_semaphore()

    def greet(off, _):
        pl.semaphore_signal(barrier, inc=1, device_id={"seq": peer_of(off)}, device_id_type=MESH)
        return 0

    lax.fori_loop(1, HEADS, greet, 0)
    pl.semaphore_signal(barrier, inc=1, device_id={"rep": right}, device_id_type=MESH)
    pl.semaphore_signal(barrier, inc=1, device_id={"rep": left}, device_id_type=MESH)
    pl.semaphore_wait(barrier, HEADS - 1 + 2)

    def a2a_copy(a, peer, slot):
        return pltpu.make_async_remote_copy(
            src_ref=ins[a].at[:, pl.ds(pl.multiple_of(peer * DIM, DIM), DIM)],
            dst_ref=rx.at[a, slot],
            send_sem=send_sem.at[a, peer], recv_sem=recv_sem.at[a, slot],
            device_id={"seq": peer}, device_id_type=MESH)

    def own_copy(a):
        return pltpu.make_async_copy(
            ins[a].at[:, pl.ds(pl.multiple_of(me * DIM, DIM), DIM)], rx.at[a, me], own_sem.at[a])

    for a in range(3):
        own_copy(a).start()

        def send(off, _):
            a2a_copy(a, peer_of(off), me).start()
            return 0

        lax.fori_loop(1, HEADS, send, 0)

    order = order_ref[...]
    block = order >> 7
    mine = (block & (REPS - 1)) == rep
    key_s[...] = jnp.where(mine, block >> 2, -1)
    low_s[...] = order & (LOCAL - 1)
    present = jnp.where(mine, 1.0, 0.0).astype(bf16)
    rows, cols = iota((128, 128), 0), iota((128, 128), 1)
    upper = jnp.where(rows < cols, 1.0, 0.0).astype(bf16)
    lower = jnp.where(cols < rows, 1.0, 0.0).astype(bf16)
    ones = jnp.ones((128, 128), bf16)
    within = jnp.dot(present, upper, preferred_element_type=f32)
    totals = jnp.dot(present, ones, preferred_element_type=f32).astype(bf16)
    rank = within + jnp.dot(lower, totals, preferred_element_type=f32)
    rank_hi = jnp.floor(rank * (1.0 / 64.0))
    rhi_s[...] = rank_hi
    rlo_s[...] = rank - 64.0 * rank_hi

    def accumulate(step, carry):
        d, dt = carry
        his, los, bs = [], [], []
        base = pl.multiple_of(step * 8, 8)
        key8, low8 = key_s[pl.ds(base, 8), :], low_s[pl.ds(base, 8), :]
        rhi8, rlo8 = rhi_s[pl.ds(base, 8), :], rlo_s[pl.ds(base, 8), :]
        for j in range(8):
            hit = iota((HEADS, 128), 0) == key8[j:j + 1]
            his.append(jnp.where(hit, rhi8[j:j + 1], 0.0))
            los.append(jnp.where(hit, rlo8[j:j + 1], 0.0))
            bs.append(jnp.where(iota((128, 128), 0) == low8[j:j + 1], 1.0, 0.0))
        left_m = jnp.concatenate([jnp.concatenate(his, 1), jnp.concatenate(los, 1)], 0).astype(bf16)
        right_m = jnp.concatenate(bs, 1).astype(bf16)
        return d + dot_nt(left_m, right_m), dt + dot_nt(right_m, left_m)

    d, dt = lax.fori_loop(0, 16, accumulate, (jnp.zeros((2 * HEADS, 128), f32), jnp.zeros((128, 2 * HEADS), f32)))
    dest_s[...] = (64.0 * d[:HEADS] + d[HEADS:]).astype(i32)
    destt_s[...] = (64.0 * dt[:, :HEADS] + dt[:, HEADS:]).astype(i32)
    dest_copy = pltpu.make_async_copy(dest_s, dest_out, out_sem.at[0])
    destt_copy = pltpu.make_async_copy(destt_s, destt_out, out_sem.at[1])
    dest_copy.start()
    destt_copy.start()

    def build(kb, _):
        base = pl.multiple_of(kb * 256, 256)
        row = iota((256, 128), 0) + base
        for s in range(HEADS):
            onehot[pl.ds(base, 256), s * 128:(s + 1) * 128] = jnp.where(
                row == dest_s[s:s + 1, :], 1.0, 0.0).astype(bf16)
        return 0

    lax.fori_loop(0, SPAN // 256, build, 0)

    def wait_in(a):
        def one(off, _):
            a2a_copy(a, me, peer_of(off)).wait_recv()
            return 0

        lax.fori_loop(1, HEADS, one, 0)
        own_copy(a).wait()

    def rows_of(c):
        return pl.ds(pl.multiple_of(c * CHUNK, CHUNK), CHUNK)

    def ycopy(a, kind, c):
        if kind == 0:
            src, slot, to = sorted_.at[a, rows_of(c)], rep, right
        elif kind == 1:
            src, slot, to = sorted_.at[a, rows_of(c)], rep, left
        else:
            even = lax.rem(c, 2) == 0
            slot = jnp.where(even, left, right)
            to = jnp.where(even, right, left)
            src = alls[a].at[slot, rows_of(c)]
        return pltpu.make_async_remote_copy(
            src_ref=src, dst_ref=alls[a].at[slot, rows_of(c)],
            send_sem=ysend.at[a, kind, c], recv_sem=yrecv.at[a, kind, c],
            device_id={"rep": to}, device_id_type=MESH)

    def keep_copy(a, c):
        to = alls[a].at[rep, rows_of(c)] if a < 2 else qs.at[rows_of(c)]
        return pltpu.make_async_copy(sorted_.at[a, rows_of(c)], to, out_sem.at[2 + a * CHUNKS + c])

    def wait_y(a, kind, c):
        if kind == 0:
            slot = left
        elif kind == 1:
            slot = right
        else:
            slot = lax.rem(rep + 2, REPS)
        pltpu.make_async_remote_copy(
            src_ref=sorted_.at[a, rows_of(c)], dst_ref=alls[a].at[slot, rows_of(c)],
            send_sem=ysend.at[a, kind, c], recv_sem=yrecv.at[a, kind, c],
            device_id={"rep": right}, device_id_type=MESH).wait_recv()

    def forward(a, c):
        wait_y(a, 0, c)
        wait_y(a, 1, c)
        ycopy(a, 2, c).start()

    for a in range(3):
        wait_in(a)

        def sort(c, _):
            sorted_[a, rows_of(c)] = jnp.dot(
                onehot[rows_of(c), :], rx[a].reshape(SPAN, DIM), preferred_element_type=f32).astype(bf16)
            if a < 2:
                ycopy(a, 0, c).start()
                ycopy(a, 1, c).start()
            keep_copy(a, c).start()
            if a > 0:
                forward(a - 1, c)
            return 0

        lax.fori_loop(0, CHUNKS, sort, 0)

    dest_copy.wait()
    destt_copy.wait()

    def finish(c, _):
        for a in range(3):
            keep_copy(a, c).wait()
        for a in range(2):
            wait_y(a, 2, c)
            for kind in range(3):
                ycopy(a, kind, c).wait_send()
        return 0

    lax.fori_loop(0, CHUNKS, finish, 0)

    def sent(off, _):
        for a in range(3):
            a2a_copy(a, peer_of(off), me).wait_send()
        return 0

    lax.fori_loop(1, HEADS, sent, 0)


def gather_call(q, k, v, order):
    any_ = pl.BlockSpec(memory_space=pl.ANY)
    vmem = pl.BlockSpec(memory_space=pltpu.VMEM)
    return pl.pallas_call(
        gather_kernel,
        out_shape=(
            jax.ShapeDtypeStruct((REPS, SPAN, DIM), bf16),
            jax.ShapeDtypeStruct((REPS, SPAN, DIM), bf16),
            jax.ShapeDtypeStruct((SPAN, DIM), bf16),
            jax.ShapeDtypeStruct((HEADS, LOCAL), i32),
            jax.ShapeDtypeStruct((LOCAL, HEADS), i32),
        ),
        in_specs=[any_, any_, any_, vmem],
        out_specs=(any_,) * 5,
        scratch_shapes=[
            pltpu.VMEM((3, HEADS, LOCAL, DIM), bf16),
            pltpu.VMEM((3, SPAN, DIM), bf16),
            pltpu.VMEM((SPAN, SPAN), bf16),
            pltpu.VMEM((128, 128), i32),
            pltpu.VMEM((128, 128), i32),
            pltpu.VMEM((128, 128), f32),
            pltpu.VMEM((128, 128), f32),
            pltpu.VMEM((HEADS, LOCAL), i32),
            pltpu.VMEM((LOCAL, HEADS), i32),
            pltpu.SemaphoreType.DMA((3, HEADS)),
            pltpu.SemaphoreType.DMA((3, HEADS)),
            pltpu.SemaphoreType.DMA((3,)),
            pltpu.SemaphoreType.DMA((2, 3, CHUNKS)),
            pltpu.SemaphoreType.DMA((2, 3, CHUNKS)),
            pltpu.SemaphoreType.DMA((2 + 3 * CHUNKS,)),
        ],
        compiler_params=pltpu.CompilerParams(
            collective_id=0, has_side_effects=True, vmem_limit_bytes=56 * 2**20),
        name="gather_sorted",
    )(q, k, v, order)


def attend_kernel(off_ref, cnt_ref, list_ref, ext_ref, rep_ref, kall, vall, qs, out, kc, vc, acc):
    def piece(c, r, start, k):
        off, n = off_ref[r, c], cnt_ref[r, c]
        lo = (off // 16) * 16 + k * WINDOW
        at = jnp.minimum(lo, SPAN - WINDOW)
        first = jnp.maximum(off, lo)
        last = jnp.minimum(off + n, lo + WINDOW)
        shift = start - off
        m = iota((CLUSTER, WINDOW), 0)
        diff = m - iota((CLUSTER, WINDOW), 1)
        hit = (diff == at + shift) & (m >= first + shift) & (m < last + shift)
        return jnp.where(hit, 1.0, 0.0).astype(bf16), pl.multiple_of(at, 16)

    def compact(c, _):
        start = jnp.int32(0)
        ones, keys, vals = [], [], []
        starts = []
        most = jnp.int32(0)
        for r in range(REPS):
            hot, at = piece(c, r, start, 0)
            ones.append(hot)
            keys.append(kall[r, pl.ds(at, WINDOW), :])
            vals.append(vall[r, pl.ds(at, WINDOW), :])
            starts.append(start)
            start = start + cnt_ref[r, c]
            most = jnp.maximum(most, off_ref[r, c] % 16 + cnt_ref[r, c])
        kv = jnp.concatenate([jnp.concatenate(keys, 0), jnp.concatenate(vals, 0)], 1)
        whole = jnp.dot(jnp.concatenate(ones, 1), kv, preferred_element_type=f32)
        rows = pl.ds(pl.multiple_of(c * CLUSTER, CLUSTER), CLUSTER)
        kc[rows, :] = whole[:, :DIM].astype(bf16)
        vc[rows, :] = whole[:, DIM:].astype(bf16)

        @pl.when(most > WINDOW)
        def _():
            for r in range(REPS):
                def more(k, _):
                    hot, at = piece(c, r, starts[r], k)
                    kc[rows, :] = (kc[rows, :].astype(f32) + jnp.dot(
                        hot, kall[r, pl.ds(at, WINDOW), :], preferred_element_type=f32)).astype(bf16)
                    vc[rows, :] = (vc[rows, :].astype(f32) + jnp.dot(
                        hot, vall[r, pl.ds(at, WINDOW), :], preferred_element_type=f32)).astype(bf16)
                    return 0

                lax.fori_loop(1, 3, more, 0)
        return 0

    lax.fori_loop(0, CLUSTERS, compact, 0)

    rep = rep_ref[0]
    factor = DIM ** -0.5 * 1.4426950408889634

    def attend(c, _):
        off, n, count = off_ref[rep, c], cnt_ref[rep, c], ext_ref[c]
        base = (off // 16) * 16
        windows = jnp.where(n > 0, (off + n - base + QROWS - 1) // QROWS, 0)

        def window(k, _):
            lo = base + k * QROWS
            at = jnp.minimum(lo, SPAN - QROWS)
            rows = pl.ds(pl.multiple_of(at, 16), QROWS)
            row = iota((QROWS, DIM), 0) + at
            live = (row >= jnp.maximum(off, lo)) & (row < jnp.minimum(off + n, lo + QROWS))

            for size in range(1, 9):
                @pl.when(count == size)
                def _():
                    query = qs[rows, :]
                    spans = [pl.ds(pl.multiple_of(list_ref[c, j] * CLUSTER, CLUSTER), CLUSTER)
                             for j in range(size)]
                    scores = [dot_nt(query, kc[spans[j], :]) for j in range(size)]
                    top = functools.reduce(jnp.maximum, scores)
                    top = jnp.max(top, axis=1, keepdims=True)
                    powers = [jnp.exp2((s - top) * factor) for s in scores]
                    total = jnp.sum(functools.reduce(jnp.add, powers), axis=1, keepdims=True)
                    mixed = functools.reduce(jnp.add, [
                        jnp.dot(powers[j].astype(bf16), vc[spans[j], :], preferred_element_type=f32)
                        for j in range(size)])
                    acc[rows, :] = jnp.where(live, mixed / total, acc[rows, :])
            return 0

        lax.fori_loop(0, windows, window, 0)
        return 0

    lax.fori_loop(0, CLUSTERS, attend, 0)

    def finish(i, _):
        rows = pl.ds(pl.multiple_of(i * 512, 512), 512)
        out[rows, :] = acc[rows, :].astype(bf16)
        return 0

    lax.fori_loop(0, SPAN // 512, finish, 0)


def attend_call(off, cnt, listed, ext, rep, kall, vall, qs):
    smem = pl.BlockSpec(memory_space=pltpu.SMEM)
    vmem = pl.BlockSpec(memory_space=pltpu.VMEM)
    return pl.pallas_call(
        attend_kernel,
        out_shape=jax.ShapeDtypeStruct((SPAN, DIM), bf16),
        in_specs=[smem] * 5 + [vmem] * 3,
        out_specs=vmem,
        scratch_shapes=[
            pltpu.VMEM((TOKENS, DIM), bf16),
            pltpu.VMEM((TOKENS, DIM), bf16),
            pltpu.VMEM((SPAN, DIM), f32),
        ],
        compiler_params=pltpu.CompilerParams(vmem_limit_bytes=48 * 2**20),
        name="attend",
    )(off, cnt, listed, ext, rep, kall, vall, qs)


HALF = HEADS // 2


def return_kernel(mixed, destt_ref, out, partner_s, both_s, onehot, tx, swap_send, swap_recv,
                  send_sem, recv_sem, own_sem):
    guide, me = lax.axis_index("guide"), lax.axis_index("seq")
    other = 1 - guide
    head_guide, head_col = me // HALF, me % HALF

    barrier = pltpu.get_barrier_semaphore()
    pl.semaphore_signal(barrier, inc=1, device_id={"guide": other}, device_id_type=MESH)

    def greet(step, _):
        i = lax.rem(head_col + step, HALF)
        pl.semaphore_signal(barrier, inc=1, device_id={"guide": head_guide, "seq": guide * HALF + i},
                            device_id_type=MESH)
        return 0

    lax.fori_loop(1, HALF, greet, 0)

    @pl.when(head_guide != guide)
    def _():
        greet(0, 0)
        pl.semaphore_wait(barrier, HALF + 1)

    @pl.when(head_guide == guide)
    def _():
        pl.semaphore_wait(barrier, HALF)

    swap = pltpu.make_async_remote_copy(
        src_ref=mixed, dst_ref=partner_s, send_sem=swap_send, recv_sem=swap_recv,
        device_id={"guide": other}, device_id_type=MESH)
    swap.start()

    destt = destt_ref[...]
    picked = jnp.where(guide == 0, destt[:, :HALF], destt[:, HALF:])
    for i in range(HALF):
        for c in range(SPAN // 512):
            onehot[i * LOCAL:(i + 1) * LOCAL, c * 512:(c + 1) * 512] = jnp.where(
                picked[:, i:i + 1] == iota((LOCAL, 512), 1) + c * 512, 1.0, 0.0).astype(bf16)
    swap.wait()

    def combine(c, _):
        rows = pl.ds(pl.multiple_of(c * 512, 512), 512)
        own = mixed[rows, :].astype(f32)
        far = partner_s[rows, :].astype(f32)
        conditioned = jnp.where(guide == 0, own, far)
        unconditioned = jnp.where(guide == 0, far, own)
        both_s[rows, :] = (unconditioned + GUIDE_SCALE * (conditioned - unconditioned)).astype(bf16)
        return 0

    lax.fori_loop(0, SPAN // 512, combine, 0)

    def place(col):
        return out.at[:, pl.ds(pl.multiple_of(col * DIM, DIM), DIM)]

    def send_copy(i):
        return pltpu.make_async_remote_copy(
            src_ref=tx.at[i], dst_ref=place(head_col), send_sem=send_sem.at[i],
            recv_sem=recv_sem.at[head_col],
            device_id={"guide": head_guide, "seq": guide * HALF + i}, device_id_type=MESH)

    def wait_copy(col):
        return pltpu.make_async_remote_copy(
            src_ref=tx.at[col], dst_ref=place(col), send_sem=send_sem.at[col],
            recv_sem=recv_sem.at[col], device_id={"guide": other}, device_id_type=MESH)

    own_copy = pltpu.make_async_copy(tx.at[head_col], place(head_col), own_sem)

    def restore(i):
        rows = pl.ds(pl.multiple_of(i * LOCAL, LOCAL), LOCAL)
        tx[i] = jnp.dot(onehot[rows, :], both_s[...], preferred_element_type=f32).astype(bf16)

    def step(j, _):
        i = lax.rem(head_col + j, HALF)
        restore(i)
        send_copy(i).start()
        return 0

    lax.fori_loop(1, HALF, step, 0)
    restore(head_col)

    @pl.when(head_guide == guide)
    def _():
        own_copy.start()

    @pl.when(head_guide != guide)
    def _():
        send_copy(head_col).start()

    def finish(j, _):
        i = lax.rem(head_col + j, HALF)
        send_copy(i).wait_send()
        wait_copy(i).wait_recv()
        return 0

    lax.fori_loop(1, HALF, finish, 0)

    @pl.when(head_guide == guide)
    def _():
        own_copy.wait()

    @pl.when(head_guide != guide)
    def _():
        send_copy(head_col).wait_send()
        wait_copy(head_col).wait_recv()


def return_call(mixed, destt):
    vmem = pl.BlockSpec(memory_space=pltpu.VMEM)
    return pl.pallas_call(
        return_kernel,
        out_shape=jax.ShapeDtypeStruct((LOCAL, HALF * DIM), bf16),
        in_specs=[vmem, vmem],
        out_specs=pl.BlockSpec(memory_space=pl.ANY),
        scratch_shapes=[
            pltpu.VMEM((SPAN, DIM), bf16),
            pltpu.VMEM((SPAN, DIM), bf16),
            pltpu.VMEM((SPAN // 2, SPAN), bf16),
            pltpu.VMEM((HALF, LOCAL, DIM), bf16),
            pltpu.SemaphoreType.DMA,
            pltpu.SemaphoreType.DMA,
            pltpu.SemaphoreType.DMA((HALF,)),
            pltpu.SemaphoreType.DMA((HALF,)),
            pltpu.SemaphoreType.DMA,
        ],
        compiler_params=pltpu.CompilerParams(
            collective_id=1, has_side_effects=True, vmem_limit_bytes=48 * 2**20),
        name="return_tokens",
    )(mixed, destt)


def on_device(queries, key_vectors, value_vectors, cluster_order, key_blocks, extents):
    order = cluster_order.reshape(128, 128)
    kall, vall, qs, dest, destt = gather_call(
        queries[0], key_vectors[0], value_vectors[0], order)
    rep_of = (cluster_order.reshape(CLUSTERS, CLUSTER) // LOCAL) % REPS
    cnt = jnp.stack([jnp.sum((rep_of == r).astype(i32), axis=1) for r in range(REPS)])
    off = jnp.cumsum(cnt, axis=1) - cnt
    rep = lax.axis_index("rep").astype(i32).reshape(1)
    mixed = attend_call(off, cnt, key_blocks[0], extents[0], rep, kall, vall, qs)
    return return_call(mixed, destt)


def solution(mesh):
    placed = (
        P("guide", ("seq", "rep"), None),
        P("guide", ("seq", "rep"), None),
        P("guide", ("seq", "rep"), None),
        P("seq", None),
        P("seq", None, None),
        P("seq", None),
    )
    return jax.shard_map(
        on_device, mesh=mesh, in_specs=placed, out_specs=P(("seq", "rep"), "guide"), check_vma=False
    )
```

time: 703 us -> 203 us (0.29)
  waiting for transfers between devices: 276 us -> 0 us
  local copies, waits for them, and re-layouts: 229 us -> 3.97 us
  Pallas kernels: 0 us -> 197 us
  blocking collectives: 108 us -> 0 us
  matrix products: 30.1 us -> 0 us
  starting transfers between devices: 28.4 us -> 0 us
  between operations: 13.3 us -> 0.07 us
  other arithmetic: 14.8 us -> 2.11 us
    pallas_call x0 -> x3, Pallas kernels: none -> 197 us  [the longest x1 110 us: gather_call(): pl.pallas_call(gather_kernel, out_shape=(jax.ShapeDtypeStruct((REPS, SPAN...]
    gather x19 -> x0, local copies, waits for them, and re-layouts: 177 us -> none  [the longest x1 58.2 us: on_device(): head_keys = jnp.take(all_keys, rows_sorted, axis=0)]
    all_gather x3 -> x0, waiting for transfers between devices: 161 us -> none  [the longest x1 55.7 us: on_device(): lax.all_gather(local_keys, 'rep', axis=0, tiled=True)]
    all_to_all x2 -> x0, blocking collectives: 108 us -> none  [the longest x1 103 us: on_device(): lax.all_to_all(pieces, 'seq', split_axis=0, concat_axis=1, tiled=True)]
    all_to_all x3 -> x0, waiting for transfers between devices: 65.8 us -> none  [the longest x1 32.9 us: on_device(): lax.all_to_all(gathered[1], 'seq', split_axis=1, concat_axis=0, tiled=True)]
    unnamed x5 -> x0, waiting for transfers between devices: 48.9 us -> none
    all_to_all x3 -> x0, starting transfers between devices: 28.1 us -> none  [the longest x1 10.2 us: on_device(): lax.all_to_all(gathered[1], 'seq', split_axis=1, concat_axis=0, tiled=True)]
    dot_general x8 -> x0, matrix products: 19 us -> none  [one_group(): jnp.einsum('gqk,gkd->gqd', weights, block_values, preferred_element_type=...]
  transfers between devices with their start and end apart: 7 -> 0, of which waited for: 6 -> 0; matrix products, arithmetic and copies ran while one was open for 19% -> 0% of each run, Pallas kernels for 0% -> 0%
where the time goes in v1:
time: 203 us
  Pallas kernels  197 us (97%)
  local copies, waits for them, and re-layouts  3.97 us (2%)
  other arithmetic  2.11 us (1%)
    pallas_call x1, Pallas kernels, gather_call(): pl.pallas_call(gather_kernel, out_shape=(jax.ShapeDtypeStruct((REPS, SPAN...  110 us
    pallas_call x1, Pallas kernels, attend_call(): pl.pallas_call(attend_kernel, out_shape=jax.ShapeDtypeStruct((SPAN, DIM),...  52.6 us
    pallas_call x1, Pallas kernels, return_call(): pl.pallas_call(return_kernel, out_shape=jax.ShapeDtypeStruct((LOCAL, HALF...  34.3 us

profile of v1, /device:TPU:6, one launch (start us, length us, event | category | flops | bytes accessed | tf_op | source)
XLA Modules:
  0.0 203.2 jit_solution(2077774627292287334)
XLA Ops:
  0.0 0.8 copy.7
  0.8 0.5 broadcast.213
  1.3 1.6 reduce.3
  3.0 0.2 convert_reduce_fusion.3
  3.2 0.2 reduce_window_sum.11
  3.4 110.1 %gather_sorted.1 = (bf16[4,4096,128]{2,1,0:T(8,128)(2,1)}, bf16[4,4096,128]{2,1,0:T(8,128)(2,1)}, bf16[4096,128]{1,0:T(8,128)(2,1)}, s32[32,128]{1,0:T(8,128)}, s32[128,32]{1,0:T(8,128)}) custom-call(bf16[128,4096]{1,0:T(8,128)(2,1)} %bitcast.13, bf16[128,4096]{1,0:T(8,128)(2,1)} %bitcast.14, bf16[128,4096]{1,0:T(8,128)(2,1)} %bitcast.15, s32[128,128]{1,0:T(8,128)} %bitcast.16), custom_call_target="tpu_custom_call" | custom-call | tf_op jit(solution)/shard_map/gather_sorted/pallas_call | solution.py:220
  113.6 0.0 copy-start
  113.6 1.2 copy-done
  114.8 0.0 copy-start.2
  114.8 0.7 copy-done.2
  115.4 0.0 copy-start.1
  115.5 52.6 %attend.1.mixed = bf16[4096,128]{1,0:T(8,128)(2,1)S(1)} custom-call(s32[4,64]{1,0:T(4,128)S(1)} %fusion.3.off_ref, s32[4,64]{1,0:T(4,128)S(1)} %pad_add_fusion.cnt_ref, s32[64,8]{1,0:T(8,128)S(1)} %bitcast.11, s32[64]{0:T(128)S(1)} %bitcast.12, s32[1]{0:T(128)} %bitcast.6.rep_ref, bf16[4,4096,128]{2,1,0:T(8,128)(2,1)} %get-tuple-element.9.kall, ...), custom_call_target="tpu_custom_call" | custom-call | tf_op jit(solution)/shard_map/attend/pallas_call | solution.py:350
  168.0 0.0 copy-done.1
  168.0 34.3 %return_tokens.1 = bf16[128,2048]{1,0:T(8,128)(2,1)S(1)} custom-call(bf16[4096,128]{1,0:T(8,128)(2,1)S(1)} %attend.1.mixed, s32[128,32]{1,0:T(8,128)S(1)} %copy-done.1), custom_call_target="tpu_custom_call" | custom-call | tf_op jit(solution)/shard_map/return_tokens/pallas_call | solution.py:475
  202.4 0.8 copy.9
  (3 shorter events, 0.0 us)
Async XLA Ops:
  113.6 1.2 copy-start
  114.8 0.7 copy-start.2
  115.4 52.6 %copy-start.1 = (s32[128,32]{1,0:T(8,128)S(1)}, s32[128,32]{1,0:T(8,128)}, u32[]{:S(2)}) copy-start(s32[128,32]{1,0:T(8,128)} %get-tuple-element.12.destt_ref) | copy-start | bytes 49156

commit v2 on v1

--- a/solution.py
+++ b/solution.py
@@ -251,90 +251,121 @@
     )(q, k, v, order)
 
 
-def attend_kernel(off_ref, cnt_ref, list_ref, ext_ref, rep_ref, kall, vall, qs, out, kc, vc, acc):
-    def piece(c, r, start, k):
-        off, n = off_ref[r, c], cnt_ref[r, c]
-        lo = (off // 16) * 16 + k * WINDOW
-        at = jnp.minimum(lo, SPAN - WINDOW)
-        first = jnp.maximum(off, lo)
-        last = jnp.minimum(off + n, lo + WINDOW)
-        shift = start - off
+GROUP = 4
+
+
+def attend_kernel(off_ref, cnt_ref, list_ref, ext_ref, perm_ref, rep_ref, kall, vall, qs, out, kc, vc, acc):
+    ones = jnp.ones((CLUSTER, DIM), bf16)
+
+    def span(c):
+        return pl.ds(pl.multiple_of(c * CLUSTER, CLUSTER), CLUSTER)
+
+    def compact_slow(c):
+        def window(k, whole):
+            start = jnp.int32(0)
+            for r in range(REPS):
+                off, n = off_ref[r, c], cnt_ref[r, c]
+                lo = (off // 16) * 16 + k * WINDOW
+                at = pl.multiple_of(jnp.minimum(lo, SPAN - WINDOW), 16)
+                first, last = jnp.maximum(off, lo), jnp.minimum(off + n, lo + WINDOW)
+                shift = start - off
+                m = iota((CLUSTER, WINDOW), 0)
+                hit = (m - iota((CLUSTER, WINDOW), 1) == at + shift) & (m >= first + shift) & (m < last + shift)
+                kv = jnp.concatenate([kall[r, pl.ds(at, WINDOW), :], vall[r, pl.ds(at, WINDOW), :]], 1)
+                whole = whole + jnp.dot(jnp.where(hit, 1.0, 0.0).astype(bf16), kv, preferred_element_type=f32)
+                start = start + n
+            return whole
+
+        whole = lax.fori_loop(0, 3, window, jnp.zeros((CLUSTER, 2 * DIM), f32))
+        kc[span(c), :] = whole[:, :DIM].astype(bf16)
+        vc[span(c), :DIM] = whole[:, DIM:].astype(bf16)
+
+    def compact_fast(c):
         m = iota((CLUSTER, WINDOW), 0)
-        diff = m - iota((CLUSTER, WINDOW), 1)
-        hit = (diff == at + shift) & (m >= first + shift) & (m < last + shift)
-        return jnp.where(hit, 1.0, 0.0).astype(bf16), pl.multiple_of(at, 16)
-
-    def compact(c, _):
-        start = jnp.int32(0)
-        ones, keys, vals = [], [], []
-        starts = []
+        start, target = jnp.int32(0), None
+        keys, vals = [], []
+        for r in range(REPS):
+            off = off_ref[r, c]
+            at = pl.multiple_of(jnp.minimum((off // 16) * 16, SPAN - WINDOW), 16)
+            moved = m + (off - at - start + r * WINDOW)
+            target = moved if r == 0 else jnp.where(m >= start, moved, target)
+            keys.append(kall[r, pl.ds(at, WINDOW), :])
+            vals.append(vall[r, pl.ds(at, WINDOW), :])
+            start = start + cnt_ref[r, c]
+        lane = iota((CLUSTER, WINDOW), 1)
+        hot = jnp.concatenate(
+            [jnp.where(target == lane + r * WINDOW, 1.0, 0.0).astype(bf16) for r in range(REPS)], 1)
+        kv = jnp.concatenate([jnp.concatenate(keys, 0), jnp.concatenate(vals, 0)], 1)
+        whole = jnp.dot(hot, kv, preferred_element_type=f32)
+        kc[span(c), :] = whole[:, :DIM].astype(bf16)
+        vc[span(c), :] = jnp.concatenate([whole[:, DIM:].astype(bf16), ones], 1)
+
+    def long_pieces(c):
         most = jnp.int32(0)
         for r in range(REPS):
-            hot, at = piece(c, r, start, 0)
-            ones.append(hot)
-            keys.append(kall[r, pl.ds(at, WINDOW), :])
-            vals.append(vall[r, pl.ds(at, WINDOW), :])
-            starts.append(start)
-            start = start + cnt_ref[r, c]
             most = jnp.maximum(most, off_ref[r, c] % 16 + cnt_ref[r, c])
-        kv = jnp.concatenate([jnp.concatenate(keys, 0), jnp.concatenate(vals, 0)], 1)
-        whole = jnp.dot(jnp.concatenate(ones, 1), kv, preferred_element_type=f32)
-        rows = pl.ds(pl.multiple_of(c * CLUSTER, CLUSTER), CLUSTER)
-        kc[rows, :] = whole[:, :DIM].astype(bf16)
-        vc[rows, :] = whole[:, DIM:].astype(bf16)
-
-        @pl.when(most > WINDOW)
-        def _():
-            for r in range(REPS):
-                def more(k, _):
-                    hot, at = piece(c, r, starts[r], k)
-                    kc[rows, :] = (kc[rows, :].astype(f32) + jnp.dot(
-                        hot, kall[r, pl.ds(at, WINDOW), :], preferred_element_type=f32)).astype(bf16)
-                    vc[rows, :] = (vc[rows, :].astype(f32) + jnp.dot(
-                        hot, vall[r, pl.ds(at, WINDOW), :], preferred_element_type=f32)).astype(bf16)
-                    return 0
-
-                lax.fori_loop(1, 3, more, 0)
-        return 0
-
-    lax.fori_loop(0, CLUSTERS, compact, 0)
+        return most > WINDOW
+
+    def compact(i, _):
+        cs = [i * GROUP + u for u in range(GROUP)]
+        for c in cs:
+            compact_fast(c)
+        for c in cs:
+            @pl.when(long_pieces(c))
+            def _():
+                compact_slow(c)
+        return 0
+
+    lax.fori_loop(0, CLUSTERS // GROUP, compact, 0)
 
     rep = rep_ref[0]
     factor = DIM ** -0.5 * 1.4426950408889634
 
-    def attend(c, _):
-        off, n, count = off_ref[rep, c], cnt_ref[rep, c], ext_ref[c]
-        base = (off // 16) * 16
-        windows = jnp.where(n > 0, (off + n - base + QROWS - 1) // QROWS, 0)
-
-        def window(k, _):
-            lo = base + k * QROWS
+    def attend_rows(cs, k, size):
+        rows, live, blocks, tops, scores = [], [], [], [], []
+        for c in cs:
+            off, n = off_ref[rep, c], cnt_ref[rep, c]
+            lo = (off // 16) * 16 + k * QROWS
             at = jnp.minimum(lo, SPAN - QROWS)
-            rows = pl.ds(pl.multiple_of(at, 16), QROWS)
+            rows.append(pl.ds(pl.multiple_of(at, 16), QROWS))
             row = iota((QROWS, DIM), 0) + at
-            live = (row >= jnp.maximum(off, lo)) & (row < jnp.minimum(off + n, lo + QROWS))
-
-            for size in range(1, 9):
-                @pl.when(count == size)
-                def _():
-                    query = qs[rows, :]
-                    spans = [pl.ds(pl.multiple_of(list_ref[c, j] * CLUSTER, CLUSTER), CLUSTER)
-                             for j in range(size)]
-                    scores = [dot_nt(query, kc[spans[j], :]) for j in range(size)]
-                    top = functools.reduce(jnp.maximum, scores)
-                    top = jnp.max(top, axis=1, keepdims=True)
-                    powers = [jnp.exp2((s - top) * factor) for s in scores]
-                    total = jnp.sum(functools.reduce(jnp.add, powers), axis=1, keepdims=True)
-                    mixed = functools.reduce(jnp.add, [
-                        jnp.dot(powers[j].astype(bf16), vc[spans[j], :], preferred_element_type=f32)
-                        for j in range(size)])
-                    acc[rows, :] = jnp.where(live, mixed / total, acc[rows, :])
-            return 0
-
-        lax.fori_loop(0, windows, window, 0)
-        return 0
-
-    lax.fori_loop(0, CLUSTERS, attend, 0)
+            live.append((row >= jnp.maximum(off, lo)) & (row < jnp.minimum(off + n, lo + QROWS)))
+            blocks.append([span(list_ref[c, jnp.where(j < ext_ref[c], j, 0)]) for j in range(size)])
+        for u in range(len(cs)):
+            query = qs[rows[u], :]
+            scores.append([dot_nt(query, kc[b, :]) for b in blocks[u]])
+        for u in range(len(cs)):
+            tops.append(jnp.max(functools.reduce(jnp.maximum, scores[u]), axis=1, keepdims=True))
+        results = []
+        for u, c in enumerate(cs):
+            mixed = None
+            for j in range(size):
+                top = tops[u] if j == 0 else jnp.where(j < ext_ref[c], tops[u], jnp.inf)
+                power = jnp.exp2((scores[u][j] - top) * factor).astype(bf16)
+                part = jnp.dot(power, vc[blocks[u][j], :], preferred_element_type=f32)
+                mixed = part if mixed is None else mixed + part
+            results.append(mixed[:, :DIM] / mixed[:, DIM:])
+        for u in range(len(cs)):
+            acc[rows[u], :] = jnp.where(live[u], results[u], acc[rows[u], :])
+
+    def attend(g, _):
+        cs = [perm_ref[g * GROUP + u] for u in range(GROUP)]
+        size_most = ext_ref[cs[-1]]
+        for size in range(1, 9):
+            @pl.when(size_most == size)
+            def _():
+                attend_rows(cs, 0, size)
+        for c in cs:
+            off, n = off_ref[rep, c], cnt_ref[rep, c]
+
+            def more(k, _):
+                attend_rows([c], k, 8)
+                return 0
+
+            lax.fori_loop(1, (off % 16 + n + QROWS - 1) // QROWS, more, 0)
+        return 0
+
+    lax.fori_loop(0, CLUSTERS // GROUP, attend, 0)
 
     def finish(i, _):
         rows = pl.ds(pl.multiple_of(i * 512, 512), 512)
@@ -344,22 +375,22 @@
     lax.fori_loop(0, SPAN // 512, finish, 0)
 
 
-def attend_call(off, cnt, listed, ext, rep, kall, vall, qs):
+def attend_call(off, cnt, listed, ext, perm, rep, kall, vall, qs):
     smem = pl.BlockSpec(memory_space=pltpu.SMEM)
     vmem = pl.BlockSpec(memory_space=pltpu.VMEM)
     return pl.pallas_call(
         attend_kernel,
         out_shape=jax.ShapeDtypeStruct((SPAN, DIM), bf16),
-        in_specs=[smem] * 5 + [vmem] * 3,
+        in_specs=[smem] * 6 + [vmem] * 3,
         out_specs=vmem,
         scratch_shapes=[
             pltpu.VMEM((TOKENS, DIM), bf16),
-            pltpu.VMEM((TOKENS, DIM), bf16),
+            pltpu.VMEM((TOKENS, 2 * DIM), bf16),
             pltpu.VMEM((SPAN, DIM), f32),
         ],
-        compiler_params=pltpu.CompilerParams(vmem_limit_bytes=48 * 2**20),
+        compiler_params=pltpu.CompilerParams(vmem_limit_bytes=56 * 2**20),
         name="attend",
-    )(off, cnt, listed, ext, rep, kall, vall, qs)
+    )(off, cnt, listed, ext, perm, rep, kall, vall, qs)
 
 
 HALF = HEADS // 2
@@ -502,7 +533,12 @@
     cnt = jnp.stack([jnp.sum((rep_of == r).astype(i32), axis=1) for r in range(REPS)])
     off = jnp.cumsum(cnt, axis=1) - cnt
     rep = lax.axis_index("rep").astype(i32).reshape(1)
-    mixed = attend_call(off, cnt, key_blocks[0], extents[0], rep, kall, vall, qs)
+    ext = extents[0]
+    index = jnp.arange(CLUSTERS, dtype=i32)
+    before = (ext[None, :] < ext[:, None]) | ((ext[None, :] == ext[:, None]) & (index[None, :] < index[:, None]))
+    place = jnp.sum(before.astype(i32), axis=1)
+    perm = jnp.sum(jnp.where(place[None, :] == index[:, None], index[None, :], 0), axis=1)
+    mixed = attend_call(off, cnt, key_blocks[0], ext, perm, rep, kall, vall, qs)
     return return_call(mixed, destt)
 
 

time: 203 us -> 179 us (0.88)
  Pallas kernels: 197 us -> 170 us
  other arithmetic: 2.11 us -> 4.24 us
    pallas_call x1, Pallas kernels: 52.6 us -> 36 us  [attend_call(): pl.pallas_call(attend_kernel, out_shape=jax.ShapeDtypeStruct((SPAN, DIM),...]
    pallas_call x1, Pallas kernels: 34.3 us -> 24.3 us  [return_call(): pl.pallas_call(return_kernel, out_shape=jax.ShapeDtypeStruct((LOCAL, HALF...]
where the time goes in v2:
time: 179 us
  Pallas kernels  170 us (95%)
  other arithmetic  4.24 us (2%)
  local copies, waits for them, and re-layouts  4.02 us (2%)
    pallas_call x1, Pallas kernels, gather_call(): pl.pallas_call(gather_kernel, out_shape=(jax.ShapeDtypeStruct((REPS, SPAN...  110 us
    pallas_call x1, Pallas kernels, attend_call(): pl.pallas_call(attend_kernel, out_shape=jax.ShapeDtypeStruct((SPAN, DIM),...  36 us
    pallas_call x1, Pallas kernels, return_call(): pl.pallas_call(return_kernel, out_shape=jax.ShapeDtypeStruct((LOCAL, HALF...  24.3 us
    unnamed x9, local copies, waits for them, and re-layouts  4 us

profile of v2, /device:TPU:6, one launch (start us, length us, event | category | flops | bytes accessed | tf_op | source)
XLA Modules:
  0.0 178.6 jit_solution(7435748271804613436)
XLA Ops:
  0.0 0.9 convert_reduce_fusion.4
  0.9 0.6 select_reduce_fusion.perm_ref
  1.6 1.4 copy.8
  2.9 0.6 broadcast.214
  3.5 1.7 reduce.3
  5.2 0.2 convert_reduce_fusion.3
  5.5 0.0 copy-start.2
  5.5 0.2 reduce_window_sum.11
  5.7 0.5 fusion.5.off_ref
  6.3 110.0 %gather_sorted.1 = (bf16[4,4096,128]{2,1,0:T(8,128)(2,1)}, bf16[4,4096,128]{2,1,0:T(8,128)(2,1)}, bf16[4096,128]{1,0:T(8,128)(2,1)}, s32[32,128]{1,0:T(8,128)}, s32[128,32]{1,0:T(8,128)}) custom-call(bf16[128,4096]{1,0:T(8,128)(2,1)} %bitcast.11, bf16[128,4096]{1,0:T(8,128)(2,1)} %bitcast.12, bf16[128,4096]{1,0:T(8,128)(2,1)} %bitcast.13, s32[128,128]{1,0:T(8,128)} %bitcast.14), custom_call_target="tpu_custom_call" | custom-call | tf_op jit(solution)/shard_map/gather_sorted/pallas_call | solution.py:220
  116.3 0.0 copy-done.2
  116.3 0.0 copy-start.1
  116.3 36.0 %attend.1.mixed = bf16[4096,128]{1,0:T(8,128)(2,1)} custom-call(s32[4,64]{1,0:T(4,128)} %fusion.5.off_ref, s32[4,64]{1,0:T(4,128)} %copy-done.2, s32[64,8]{1,0:T(8,128)} %bitcast.15, s32[64]{0:T(128)} %bitcast.25, s32[64]{0:T(128)} %select_reduce_fusion.perm_ref, s32[1]{0:T(128)} %bitcast.6.rep_ref, bf16[4,4096,128]{2,1,0:T(8,128)(2,1)} %get-tuple-element.9.kall, ...), custom_call_target="tpu_custom_call" | custom-call | tf_op jit(solution)/shard_map/attend/pallas_call | solution.py:381
  152.3 0.0 copy-done.1
  152.3 0.0 copy-start
  152.3 1.2 copy-done
  153.5 24.3 %return_tokens.1 = bf16[128,2048]{1,0:T(8,128)(2,1)S(1)} custom-call(bf16[4096,128]{1,0:T(8,128)(2,1)S(1)} %copy-done, s32[128,32]{1,0:T(8,128)S(1)} %copy-done.1), custom_call_target="tpu_custom_call" | custom-call | tf_op jit(solution)/shard_map/return_tokens/pallas_call | solution.py:506
  177.8 0.8 copy.10
  (2 shorter events, 0.0 us)
Async XLA Ops:
  5.5 110.8 %copy-start.2 = (s32[4,64]{1,0:T(4,128)}, s32[4,64]{1,0:T(4,128)S(1)}, u32[]{:S(2)}) copy-start(s32[4,64]{1,0:T(4,128)S(1)} %pad_add_fusion.cnt_ref) | copy-start | bytes 3076
  116.3 36.0 %copy-start.1 = (s32[128,32]{1,0:T(8,128)S(1)}, s32[128,32]{1,0:T(8,128)}, u32[]{:S(2)}) copy-start(s32[128,32]{1,0:T(8,128)} %get-tuple-element.12.destt_ref) | copy-start | bytes 49156
  152.3 1.2 copy-start

commit v3 on v2

v3 whole, which is shorter than its diff:
```python
import functools

import jax
import jax.numpy as jnp
from jax import lax
from jax.experimental import pallas as pl
from jax.experimental.pallas import tpu as pltpu
from jax.sharding import PartitionSpec as P

MESH = pl.DeviceIdType.MESH
CLUSTER = 256
GUIDE_SCALE = 5.0
HEADS = 32
SEQ_X, SEQ_Z = 4, 8
REPS = 4
TOKENS = 16384
DIM = 128
SPAN = TOKENS // REPS
LOCAL = 128
CLUSTERS = TOKENS // CLUSTER
CHUNK = 512
CHUNKS = SPAN // CHUNK
GROUPS = 2
SLOTS = HEADS // GROUPS
LIST = SPAN // GROUPS
WINDOW = 64
QROWS = 96
f32, bf16, i32 = jnp.float32, jnp.bfloat16, jnp.int32

NT = (((1,), (1,)), ((), ()))


def dot_nt(a, b):
    return lax.dot_general(a, b, NT, preferred_element_type=f32)


def iota(shape, dim):
    return lax.broadcasted_iota(i32, shape, dim)


def z_distance(group, i):
    return i + (i // 2) * 2 + (i // 3) * 2 if group == 0 else i + 2 + i // 2


def gather_kernel(q_in, k_in, v_in, order_in, ext_ref, kall, vall, qs, table_out, destt_out,
                  rx, sorted_, onehot, order_s, key_s, low_s, rank_s, dest_s, destt_s, table_s,
                  send_sem, recv_sem, own_sem, order_sem, ysend, yrecv, keep_sem, out_sem):
    me = lax.axis_index("seq")
    rep = lax.axis_index("rep")
    x, z = me // SEQ_Z, me % SEQ_Z
    right, left = lax.rem(rep + 1, REPS), lax.rem(rep + REPS - 1, REPS)
    ins = (k_in, v_in, q_in)
    alls = (kall, vall)

    def at_distance(group, slot, sign):
        dx, dz = slot // 4, z_distance(group, slot % 4)
        return lax.rem(x + sign * dx + SEQ_X, SEQ_X) * SEQ_Z + lax.rem(z + sign * dz + SEQ_Z, SEQ_Z)

    def order_copy(u):
        return pltpu.make_async_copy(
            order_in.at[:, pl.ds(pl.multiple_of(u * 128, 128), 128)], order_s.at[pl.ds(u, 1), :], order_sem.at[u])

    def fetch(u, _):
        order_copy(u).start()
        return 0

    lax.fori_loop(0, 128, fetch, 0)

    barrier = pltpu.get_barrier_semaphore()
    for group in range(GROUPS):
        def greet(slot, _):
            pl.semaphore_signal(barrier, inc=1, device_id={"seq": at_distance(group, slot, 1)}, device_id_type=MESH)
            return 0

        lax.fori_loop(1 - group, SLOTS, greet, 0)
    pl.semaphore_signal(barrier, inc=1, device_id={"rep": right}, device_id_type=MESH)
    pl.semaphore_signal(barrier, inc=1, device_id={"rep": left}, device_id_type=MESH)
    pl.semaphore_wait(barrier, HEADS - 1 + 2)

    def a2a_copy(a, group, slot):
        peer = at_distance(group, slot, 1)
        return pltpu.make_async_remote_copy(
            src_ref=ins[a].at[:, pl.ds(pl.multiple_of(peer * DIM, DIM), DIM)],
            dst_ref=rx.at[a, group, pl.ds(pl.multiple_of(slot * LOCAL, LOCAL), LOCAL)],
            send_sem=send_sem.at[a, group, slot], recv_sem=recv_sem.at[a, group, slot],
            device_id={"seq": peer}, device_id_type=MESH)

    def own_copy(a):
        return pltpu.make_async_copy(
            ins[a].at[:, pl.ds(pl.multiple_of(me * DIM, DIM), DIM)], rx.at[a, 0, pl.ds(0, LOCAL)], own_sem.at[a])

    for a in range(3):
        own_copy(a).start()
        for group in range(GROUPS):
            def send(slot, _):
                a2a_copy(a, group, slot).start()
                return 0

            lax.fori_loop(1 - group, SLOTS, send, 0)

    def fetched(u, _):
        order_copy(u).wait()
        return 0

    lax.fori_loop(0, 128, fetched, 0)

    order = order_s[...]
    block = order >> 7
    owner = block & (REPS - 1)
    away = (z - (block >> 2)) & (SEQ_Z - 1)
    second = jnp.where((away == 0) | (away == 1) | (away == 4) | (away == 7), 0, 1)
    mine = owner == rep
    rows, cols = iota((128, 128), 0), iota((128, 128), 1)
    as_mask = lambda hit: jnp.where(hit, 1.0, 0.0).astype(bf16)
    product = lambda a, b: jnp.dot(a, b, preferred_element_type=f32)
    upper, lower = as_mask(rows < cols), as_mask(cols < rows)
    to_cluster, past_cluster = as_mask(cols < (rows >> 1) * 2), as_mask(cols < (rows >> 1) * 2 + 2)
    ones = jnp.ones((128, 128), bf16)
    ranks, befores, pasts = [], [], []
    for group in range(GROUPS):
        present = as_mask(mine & (second == group))
        totals = product(present, ones).astype(bf16)
        ranks.append(product(present, upper) + product(lower, totals))
        befores.append(product(to_cluster, totals))
        pasts.append(product(past_cluster, totals))
    rank = jnp.where(second == 0, ranks[0], ranks[1])
    whole = jnp.where(second == 0, ranks[0] + befores[1], ranks[1] + pasts[0])
    rank_hi, whole_hi = jnp.floor(rank * (1.0 / 64.0)), jnp.floor(whole * (1.0 / 64.0))
    key_s[...] = jnp.where(mine, block >> 2, -1)
    low_s[...] = order & (LOCAL - 1)
    rank_s[0] = rank_hi
    rank_s[1] = rank - 64.0 * rank_hi
    rank_s[2] = whole_hi
    rank_s[3] = whole - 64.0 * whole_hi

    def accumulate(step, carry):
        d, dt = carry
        parts, bs = [[], [], [], []], []
        base = pl.multiple_of(step * 32, 32)
        key8, low8 = key_s[pl.ds(base, 32), :], low_s[pl.ds(base, 32), :]
        rank8 = [rank_s[i, pl.ds(base, 32), :] for i in range(4)]
        for j in range(32):
            hit = iota((HEADS, 128), 0) == key8[j:j + 1]
            for i in range(4):
                parts[i].append(jnp.where(hit, rank8[i][j:j + 1], 0.0).astype(bf16))
            bs.append(as_mask(iota((128, 128), 0) == low8[j:j + 1]))
        parts = [jnp.concatenate(p, 1) for p in parts]
        right_m = jnp.concatenate(bs, 1)
        d = d + dot_nt(jnp.concatenate(parts[:2], 0), right_m)
        dt = dt + dot_nt(right_m, jnp.concatenate(parts[2:], 0))
        return d, dt

    d, dt = lax.fori_loop(0, 4, accumulate, (jnp.zeros((2 * HEADS, 128), f32), jnp.zeros((128, 2 * HEADS), f32)))
    dest_s[...] = (64.0 * d[:HEADS] + d[HEADS:]).astype(i32)
    destt_s[...] = (64.0 * dt[:, :HEADS] + dt[:, HEADS:]).astype(i32)

    def build(group):
        for slot in range(SLOTS):
            row = dest_s[pl.ds(at_distance(group, slot, -1), 1), :]

            def block_of(kb, _):
                base = pl.multiple_of(kb * 256, 256)
                onehot[group, pl.ds(base, 256), slot * 128:(slot + 1) * 128] = as_mask(
                    iota((256, 128), 0) + base == row)
                return 0

            lax.fori_loop(0, LIST // 256, block_of, 0)

    def tables():
        listed = jnp.zeros((128, 128), f32)
        for r in range(REPS):
            for group in range(GROUPS):
                listed = listed + product(
                    as_mask((owner == r) & (second == group)), as_mask(cols == r * GROUPS + group))
        pair = as_mask((iota((CLUSTERS, 128), 1) >> 1) == iota((CLUSTERS, 128), 0))
        counts = product(pair, listed.astype(bf16))
        before = as_mask(iota((CLUSTERS, CLUSTERS), 1) < iota((CLUSTERS, CLUSTERS), 0))
        offsets = product(before, counts.astype(bf16))
        table_s[0:CLUSTERS, :] = counts.astype(i32)
        table_s[CLUSTERS:2 * CLUSTERS, :] = offsets.astype(i32)
        c_row, c_col = iota((CLUSTERS, CLUSTERS), 1), iota((CLUSTERS, CLUSTERS), 0)
        ext_row = ext_ref[...]
        ext_col = dot_nt(as_mask(c_row == c_col), jnp.broadcast_to(ext_row, (8, CLUSTERS)).astype(f32).astype(bf16))
        ext_col = ext_col[:, 0:1].astype(i32)
        earlier = (ext_row < ext_col) | ((ext_row == ext_col) & (c_row < c_col))
        place = jnp.sum(jnp.where(earlier, 1.0, 0.0), axis=1, keepdims=True).astype(i32)
        hit = as_mask(place == iota((CLUSTERS, 128), 1))
        table_s[2 * CLUSTERS:2 * CLUSTERS + 8, :] = product(
            iota((8, CLUSTERS), 1).astype(f32).astype(bf16), hit).astype(i32)

    def wait_in(a, group):
        def one(slot, _):
            a2a_copy(a, group, slot).wait_recv()
            return 0

        lax.fori_loop(1 - group, SLOTS, one, 0)
        if group == 0:
            own_copy(a).wait()

    def rows_of(c):
        return pl.ds(pl.multiple_of(c * CHUNK, CHUNK), CHUNK)

    def ycopy(a, kind, c):
        if kind == 0:
            src, slot, to = sorted_.at[a, rows_of(c)], rep, right
        elif kind == 1:
            src, slot, to = sorted_.at[a, rows_of(c)], rep, left
        else:
            even = lax.rem(c, 2) == 0
            slot = jnp.where(even, left, right)
            to = jnp.where(even, right, left)
            src = alls[a].at[slot, rows_of(c)]
        return pltpu.make_async_remote_copy(
            src_ref=src, dst_ref=alls[a].at[slot, rows_of(c)],
            send_sem=ysend.at[a, kind, c], recv_sem=yrecv.at[a, kind, c],
            device_id={"rep": to}, device_id_type=MESH)

    def keep_copy(a, c):
        to = alls[a].at[rep, rows_of(c)] if a < 2 else qs.at[rows_of(c)]
        return pltpu.make_async_copy(sorted_.at[a, rows_of(c)], to, keep_sem.at[a, c])

    def wait_y(a, kind, c):
        slot = (left, right, lax.rem(rep + 2, REPS))[kind]
        pltpu.make_async_remote_copy(
            src_ref=sorted_.at[a, rows_of(c)], dst_ref=alls[a].at[slot, rows_of(c)],
            send_sem=ysend.at[a, kind, c], recv_sem=yrecv.at[a, kind, c],
            device_id={"rep": right}, device_id_type=MESH).wait_recv()

    per_group = CHUNKS // GROUPS
    table_copy = pltpu.make_async_copy(table_s, table_out, out_sem.at[0])
    destt_copy = pltpu.make_async_copy(destt_s, destt_out, out_sem.at[1])
    for a in range(3):
        for group in range(GROUPS):
            if a == 0:
                build(group)
            wait_in(a, group)

            def sort(i, _):
                c = group * per_group + i
                sorted_[a, rows_of(c)] = jnp.dot(
                    onehot[group, rows_of(i), :], rx[a, group], preferred_element_type=f32).astype(bf16)
                if a < 2:
                    ycopy(a, 0, c).start()
                    ycopy(a, 1, c).start()
                keep_copy(a, c).start()
                return 0

            lax.fori_loop(0, per_group, sort, 0)
            if a == 0 and group == 0:
                tables()
                table_copy.start()
                destt_copy.start()
            if a < 2:
                def forward(i, _):
                    c = group * per_group + i
                    wait_y(a, 0, c)
                    wait_y(a, 1, c)
                    ycopy(a, 2, c).start()
                    return 0

                lax.fori_loop(0, per_group, forward, 0)

    table_copy.wait()
    destt_copy.wait()

    def finish(c, _):
        for a in range(3):
            keep_copy(a, c).wait()
        for a in range(2):
            wait_y(a, 2, c)
            for kind in range(3):
                ycopy(a, kind, c).wait_send()
        return 0

    lax.fori_loop(0, CHUNKS, finish, 0)

    for a in range(3):
        for group in range(GROUPS):
            def sent(slot, _):
                a2a_copy(a, group, slot).wait_send()
                return 0

            lax.fori_loop(1 - group, SLOTS, sent, 0)


def gather_call(q, k, v, order, ext):
    any_ = pl.BlockSpec(memory_space=pl.ANY)
    vmem = pl.BlockSpec(memory_space=pltpu.VMEM)
    return pl.pallas_call(
        gather_kernel,
        out_shape=(
            jax.ShapeDtypeStruct((REPS, SPAN, DIM), bf16),
            jax.ShapeDtypeStruct((REPS, SPAN, DIM), bf16),
            jax.ShapeDtypeStruct((SPAN, DIM), bf16),
            jax.ShapeDtypeStruct((2 * CLUSTERS + 8, 128), i32),
            jax.ShapeDtypeStruct((LOCAL, HEADS), i32),
        ),
        in_specs=[any_, any_, any_, any_, vmem],
        out_specs=(any_,) * 5,
        scratch_shapes=[
            pltpu.VMEM((3, GROUPS, LIST, DIM), bf16),
            pltpu.VMEM((3, SPAN, DIM), bf16),
            pltpu.VMEM((GROUPS, LIST, LIST), bf16),
            pltpu.VMEM((128, 128), i32),
            pltpu.VMEM((128, 128), i32),
            pltpu.VMEM((128, 128), i32),
            pltpu.VMEM((4, 128, 128), f32),
            pltpu.VMEM((HEADS, LOCAL), i32),
            pltpu.VMEM((LOCAL, HEADS), i32),
            pltpu.VMEM((2 * CLUSTERS + 8, 128), i32),
            pltpu.SemaphoreType.DMA((3, GROUPS, SLOTS)),
            pltpu.SemaphoreType.DMA((3, GROUPS, SLOTS)),
            pltpu.SemaphoreType.DMA((3,)),
            pltpu.SemaphoreType.DMA((128,)),
            pltpu.SemaphoreType.DMA((2, 3, CHUNKS)),
            pltpu.SemaphoreType.DMA((2, 3, CHUNKS)),
            pltpu.SemaphoreType.DMA((3, CHUNKS)),
            pltpu.SemaphoreType.DMA((2,)),
        ],
        compiler_params=pltpu.CompilerParams(
            collective_id=0, has_side_effects=True, vmem_limit_bytes=56 * 2**20),
        name="gather_sorted",
    )(q, k, v, order, ext)


GROUP = 4


def attend_kernel(table, list_ref, ext_ref, rep_ref, kall, vall, qs, out, kc, vc, acc):
    ones = jnp.ones((CLUSTER, DIM), bf16)
    rep = rep_ref[0]

    def span(c):
        return pl.ds(pl.multiple_of(c * CLUSTER, CLUSTER), CLUSTER)

    def extent_of(c, r, group):
        return table[CLUSTERS + c, r * GROUPS + group], table[c, r * GROUPS + group]

    def picked(c, r, k, start):
        lane = iota((1, 128), 1)
        ats, shifts, lows, highs = [], [], [], []
        for group in range(GROUPS):
            off, n = extent_of(c, r, group)
            lo = (off // 16) * 16 + k * WINDOW
            at = jnp.minimum(lo, LIST - WINDOW)
            first = start + jnp.maximum(lo - off, 0)
            last = start + jnp.minimum(n, lo + WINDOW - off)
            ats.append(pl.multiple_of(at, 16))
            shifts.append(start + at - off - group * WINDOW)
            lows.append(first)
            highs.append(last)
            start = start + n
        is_first = lane < WINDOW
        place = lane + jnp.where(is_first, shifts[0], shifts[1])
        inside = (place >= jnp.where(is_first, lows[0], lows[1])) & (place < jnp.where(is_first, highs[0], highs[1]))
        return ats, jnp.where(inside, place, -1), start

    def windows_of(ref, ats, r):
        return [ref[r, pl.ds(ats[g] + g * LIST, WINDOW), :] for g in range(GROUPS)]

    def hot(place, rows, base=0):
        return jnp.where(iota((rows, 128), 0) + base == place, 1.0, 0.0).astype(bf16)

    def join(c, k):
        start = jnp.int32(0)
        hots, keys, vals = [], [], []
        for r in range(REPS):
            ats, place, start = picked(c, r, k, start)
            hots.append(hot(place, CLUSTER))
            keys += windows_of(kall, ats, r)
            vals += windows_of(vall, ats, r)
        kv = jnp.concatenate([jnp.concatenate(keys, 0), jnp.concatenate(vals, 0)], 1)
        return jnp.dot(jnp.concatenate(hots, 1), kv, preferred_element_type=f32)

    def store(c, whole):
        kc[span(c), :] = whole[:, :DIM].astype(bf16)
        vc[span(c), :] = jnp.concatenate([whole[:, DIM:].astype(bf16), ones], 1)

    def rounds(c, r):
        most = jnp.int32(0)
        for group in range(GROUPS):
            off, n = extent_of(c, r, group)
            most = jnp.maximum(most, off % 16 + n)
        return (most + WINDOW - 1) // WINDOW

    def compact(i, _):
        cs = [i * GROUP + u for u in range(GROUP)]
        for c in cs:
            store(c, join(c, 0))
        for c in cs:
            most = functools.reduce(jnp.maximum, [rounds(c, r) for r in range(REPS)])

            @pl.when(most > 1)
            def _():
                store(c, lax.fori_loop(0, most, lambda k, whole: whole + join(c, k),
                                       jnp.zeros((CLUSTER, 2 * DIM), f32)))
        return 0

    lax.fori_loop(0, CLUSTERS // GROUP, compact, 0)

    factor = DIM ** -0.5 * 1.4426950408889634

    def queries_of(c):
        off0, n0 = extent_of(c, rep, 0)
        off1, n1 = extent_of(c, rep, 1)
        return off0 + off1, n0 + n1

    def pick_queries(c, at, off, k):
        ats, place, _ = picked(c, rep, k, off)
        rows = [qs[pl.ds(ats[g] + g * LIST, WINDOW), :] for g in range(GROUPS)]
        return jnp.dot(hot(place, QROWS, at), jnp.concatenate(rows, 0), preferred_element_type=f32)

    def attend_rows(cs, k, size, slow):
        rows, live, blocks, tops, scores, queries = [], [], [], [], [], []
        for c in cs:
            off, n = queries_of(c)
            lo = (off // 16) * 16 + k * QROWS
            at = jnp.minimum(lo, SPAN - QROWS)
            rows.append(pl.ds(pl.multiple_of(at, 16), QROWS))
            row = iota((QROWS, DIM), 0) + at
            live.append((row >= jnp.maximum(off, lo)) & (row < jnp.minimum(off + n, lo + QROWS)))
            blocks.append([span(list_ref[c, jnp.where(j < ext_ref[c], j, 0)]) for j in range(size)])
            if slow:
                query = lax.fori_loop(0, rounds(c, rep), lambda i, q: q + pick_queries(c, at, off, i),
                                      jnp.zeros((QROWS, DIM), f32))
            else:
                query = pick_queries(c, at, off, 0)
            queries.append(query.astype(bf16))
        for u in range(len(cs)):
            scores.append([dot_nt(queries[u], kc[b, :]) for b in blocks[u]])
        for u in range(len(cs)):
            tops.append(jnp.max(functools.reduce(jnp.maximum, scores[u]), axis=1, keepdims=True))
        results = []
        for u, c in enumerate(cs):
            mixed = None
            for j in range(size):
                top = tops[u] if j == 0 else jnp.where(j < ext_ref[c], tops[u], jnp.inf)
                power = jnp.exp2((scores[u][j] - top) * factor).astype(bf16)
                part = jnp.dot(power, vc[blocks[u][j], :], preferred_element_type=f32)
                mixed = part if mixed is None else mixed + part
            results.append(mixed[:, :DIM] / mixed[:, DIM:])
        for u in range(len(cs)):
            acc[rows[u], :] = jnp.where(live[u], results[u], acc[rows[u], :])

    def attend(g, _):
        cs = [table[2 * CLUSTERS, g * GROUP + u] for u in range(GROUP)]
        size_most = ext_ref[cs[-1]]
        for size in range(1, 9):
            @pl.when(size_most == size)
            def _():
                attend_rows(cs, 0, size, False)
        for c in cs:
            off, n = queries_of(c)

            def more(k, _):
                attend_rows([c], k, 8, True)
                return 0

            lax.fori_loop(jnp.where(rounds(c, rep) > 1, 0, 1), (off % 16 + n + QROWS - 1) // QROWS, more, 0)
        return 0

    lax.fori_loop(0, CLUSTERS // GROUP, attend, 0)

    def finish(i, _):
        rows = pl.ds(pl.multiple_of(i * 512, 512), 512)
        out[rows, :] = acc[rows, :].astype(bf16)
        return 0

    lax.fori_loop(0, SPAN // 512, finish, 0)


def attend_call(table, listed, ext, rep, kall, vall, qs):
    smem = pl.BlockSpec(memory_space=pltpu.SMEM)
    vmem = pl.BlockSpec(memory_space=pltpu.VMEM)
    return pl.pallas_call(
        attend_kernel,
        out_shape=jax.ShapeDtypeStruct((SPAN, DIM), bf16),
        in_specs=[smem] * 4 + [vmem] * 3,
        out_specs=vmem,
        scratch_shapes=[
            pltpu.VMEM((TOKENS, DIM), bf16),
            pltpu.VMEM((TOKENS, 2 * DIM), bf16),
            pltpu.VMEM((SPAN, DIM), f32),
        ],
        compiler_params=pltpu.CompilerParams(vmem_limit_bytes=56 * 2**20),
        name="attend",
    )(table, listed, ext, rep, kall, vall, qs)


HALF = HEADS // 2


def return_kernel(mixed, destt_ref, out, partner_s, both_s, onehot, tx, swap_send, swap_recv,
                  send_sem, recv_sem, own_sem):
    guide, me = lax.axis_index("guide"), lax.axis_index("seq")
    other = 1 - guide
    head_guide, head_col = me // HALF, me % HALF

    barrier = pltpu.get_barrier_semaphore()
    pl.semaphore_signal(barrier, inc=1, device_id={"guide": other}, device_id_type=MESH)

    def greet(step, _):
        i = lax.rem(head_col + step, HALF)
        pl.semaphore_signal(barrier, inc=1, device_id={"guide": head_guide, "seq": guide * HALF + i},
                            device_id_type=MESH)
        return 0

    lax.fori_loop(1, HALF, greet, 0)

    @pl.when(head_guide != guide)
    def _():
        greet(0, 0)
        pl.semaphore_wait(barrier, HALF + 1)

    @pl.when(head_guide == guide)
    def _():
        pl.semaphore_wait(barrier, HALF)

    swap = pltpu.make_async_remote_copy(
        src_ref=mixed, dst_ref=partner_s, send_sem=swap_send, recv_sem=swap_recv,
        device_id={"guide": other}, device_id_type=MESH)
    swap.start()

    destt = destt_ref[...]
    picked = jnp.where(guide == 0, destt[:, :HALF], destt[:, HALF:])
    for i in range(HALF):
        for c in range(SPAN // 512):
            onehot[i * LOCAL:(i + 1) * LOCAL, c * 512:(c + 1) * 512] = jnp.where(
                picked[:, i:i + 1] == iota((LOCAL, 512), 1) + c * 512, 1.0, 0.0).astype(bf16)
    swap.wait()

    def combine(c, _):
        rows = pl.ds(pl.multiple_of(c * 512, 512), 512)
        own = mixed[rows, :].astype(f32)
        far = partner_s[rows, :].astype(f32)
        conditioned = jnp.where(guide == 0, own, far)
        unconditioned = jnp.where(guide == 0, far, own)
        both_s[rows, :] = (unconditioned + GUIDE_SCALE * (conditioned - unconditioned)).astype(bf16)
        return 0

    lax.fori_loop(0, SPAN // 512, combine, 0)

    def place(col):
        return out.at[:, pl.ds(pl.multiple_of(col * DIM, DIM), DIM)]

    def send_copy(i):
        return pltpu.make_async_remote_copy(
            src_ref=tx.at[i], dst_ref=place(head_col), send_sem=send_sem.at[i],
            recv_sem=recv_sem.at[head_col],
            device_id={"guide": head_guide, "seq": guide * HALF + i}, device_id_type=MESH)

    def wait_copy(col):
        return pltpu.make_async_remote_copy(
            src_ref=tx.at[col], dst_ref=place(col), send_sem=send_sem.at[col],
            recv_sem=recv_sem.at[col], device_id={"guide": other}, device_id_type=MESH)

    own_copy = pltpu.make_async_copy(tx.at[head_col], place(head_col), own_sem)

    def restore(i):
        rows = pl.ds(pl.multiple_of(i * LOCAL, LOCAL), LOCAL)
        tx[i] = jnp.dot(onehot[rows, :], both_s[...], preferred_element_type=f32).astype(bf16)

    def step(j, _):
        i = lax.rem(head_col + j, HALF)
        restore(i)
        send_copy(i).start()
        return 0

    lax.fori_loop(1, HALF, step, 0)
    restore(head_col)

    @pl.when(head_guide == guide)
    def _():
        own_copy.start()

    @pl.when(head_guide != guide)
    def _():
        send_copy(head_col).start()

    def finish(j, _):
        i = lax.rem(head_col + j, HALF)
        send_copy(i).wait_send()
        wait_copy(i).wait_recv()
        return 0

    lax.fori_loop(1, HALF, finish, 0)

    @pl.when(head_guide == guide)
    def _():
        own_copy.wait()

    @pl.when(head_guide != guide)
    def _():
        send_copy(head_col).wait_send()
        wait_copy(head_col).wait_recv()


def return_call(mixed, destt):
    vmem = pl.BlockSpec(memory_space=pltpu.VMEM)
    return pl.pallas_call(
        return_kernel,
        out_shape=jax.ShapeDtypeStruct((LOCAL, HALF * DIM), bf16),
        in_specs=[vmem, vmem],
        out_specs=pl.BlockSpec(memory_space=pl.ANY),
        scratch_shapes=[
            pltpu.VMEM((SPAN, DIM), bf16),
            pltpu.VMEM((SPAN, DIM), bf16),
            pltpu.VMEM((SPAN // 2, SPAN), bf16),
            pltpu.VMEM((HALF, LOCAL, DIM), bf16),
            pltpu.SemaphoreType.DMA,
            pltpu.SemaphoreType.DMA,
            pltpu.SemaphoreType.DMA((HALF,)),
            pltpu.SemaphoreType.DMA((HALF,)),
            pltpu.SemaphoreType.DMA,
        ],
        compiler_params=pltpu.CompilerParams(
            collective_id=1, has_side_effects=True, vmem_limit_bytes=48 * 2**20),
        name="return_tokens",
    )(mixed, destt)


def on_device(queries, key_vectors, value_vectors, cluster_order, key_blocks, extents):
    kall, vall, qs, table, destt = gather_call(
        queries[0], key_vectors[0], value_vectors[0], cluster_order, extents)
    rep = lax.axis_index("rep").astype(i32).reshape(1)
    mixed = attend_call(table, key_blocks[0], extents[0], rep, kall, vall, qs)
    return return_call(mixed, destt)


def solution(mesh):
    placed = (
        P("guide", ("seq", "rep"), None),
        P("guide", ("seq", "rep"), None),
        P("guide", ("seq", "rep"), None),
        P("seq", None),
        P("seq", None, None),
        P("seq", None),
    )
    return jax.shard_map(
        on_device, mesh=mesh, in_specs=placed, out_specs=P(("seq", "rep"), "guide"), check_vma=False
    )
```

time: 179 us -> 173 us (0.966)
  other arithmetic: 4.24 us -> 0 us
    pallas_call x1, Pallas kernels: 24.3 us -> 34.8 us  [return_call(): pl.pallas_call(return_kernel, out_shape=jax.ShapeDtypeStruct((LOCAL, HALF...]
    pallas_call x1, Pallas kernels: 110 us -> 101 us  [gather_call(): pl.pallas_call(gather_kernel, out_shape=(jax.ShapeDtypeStruct((REPS, SPAN...]
    pallas_call x1, Pallas kernels: 36 us -> 34 us  [attend_call(): pl.pallas_call(attend_kernel, out_shape=jax.ShapeDtypeStruct((SPAN, DIM),...]
    unnamed x9 -> x6, local copies, waits for them, and re-layouts: 4 us -> 3.41 us
where the time goes in v3:
time: 173 us
  Pallas kernels  170 us (98%)
  local copies, waits for them, and re-layouts  3.41 us (2%)
    pallas_call x1, Pallas kernels, gather_call(): pl.pallas_call(gather_kernel, out_shape=(jax.ShapeDtypeStruct((REPS, SPAN...  101 us
    pallas_call x1, Pallas kernels, return_call(): pl.pallas_call(return_kernel, out_shape=jax.ShapeDtypeStruct((LOCAL, HALF...  34.8 us
    pallas_call x1, Pallas kernels, attend_call(): pl.pallas_call(attend_kernel, out_shape=jax.ShapeDtypeStruct((SPAN, DIM),...  34 us

profile of v3, /device:TPU:6, one launch (start us, length us, event | category | flops | bytes accessed | tf_op | source)
XLA Modules:
  0.0 173.0 jit_solution(2236084594284249878)
XLA Ops:
  0.0 1.4 copy.7
  1.4 100.8 %gather_sorted.1 = (bf16[4,4096,128]{2,1,0:T(8,128)(2,1)}, bf16[4,4096,128]{2,1,0:T(8,128)(2,1)}, bf16[4096,128]{1,0:T(8,128)(2,1)}, s32[136,128]{1,0:T(8,128)}, s32[128,32]{1,0:T(8,128)}) custom-call(bf16[128,4096]{1,0:T(8,128)(2,1)} %bitcast.6, bf16[128,4096]{1,0:T(8,128)(2,1)} %bitcast.7, bf16[128,4096]{1,0:T(8,128)(2,1)} %bitcast.8, ...), custom_call_target="tpu_custom_call" | custom-call | tf_op jit(solution)/shard_map/gather_sorted/pallas_call | solution.py:289
  102.2 0.0 copy-start.1
  102.2 34.0 %attend.1.mixed = bf16[4096,128]{1,0:T(8,128)(2,1)} custom-call(s32[136,128]{1,0:T(8,128)} %get-tuple-element.10.table, s32[64,8]{1,0:T(8,128)} %bitcast.9, s32[64]{0:T(128)} %bitcast.10, s32[1]{0:T(128)} %bitcast.5.rep_ref, bf16[4,4096,128]{2,1,0:T(8,128)(2,1)} %get-tuple-element.11.kall, bf16[4,4096,128]{2,1,0:T(8,128)(2,1)} %get-tuple-element.12.vall, ...), custom_call_target="tpu_custom_call" | custom-call | tf_op jit(solution)/shard_map/attend/pallas_call | solution.py:475
  136.2 0.0 copy-done.1
  136.2 0.0 copy-start
  136.2 1.2 copy-done
  137.5 34.8 %return_tokens.1 = bf16[128,2048]{1,0:T(8,128)(2,1)S(1)} custom-call(bf16[4096,128]{1,0:T(8,128)(2,1)S(1)} %copy-done, s32[128,32]{1,0:T(8,128)S(1)} %copy-done.1), custom_call_target="tpu_custom_call" | custom-call | tf_op jit(solution)/shard_map/return_tokens/pallas_call | solution.py:600
  172.2 0.8 copy.9
Async XLA Ops:
  102.2 34.0 %copy-start.1 = (s32[128,32]{1,0:T(8,128)S(1)}, s32[128,32]{1,0:T(8,128)}, u32[]{:S(2)}) copy-start(s32[128,32]{1,0:T(8,128)} %get-tuple-element.14.destt_ref) | copy-start | bytes 49156
  136.2 1.2 copy-start

commit v4 on v3

--- a/solution.py
+++ b/solution.py
@@ -24,6 +24,9 @@
 SLOTS = HEADS // GROUPS
 LIST = SPAN // GROUPS
 WINDOW = 64
+LISTS = REPS * GROUPS
+T_OVER, T_OFF_Q, T_N_Q, T_AT_Q, T_OVER_Q, T_WINDOWS_Q, T_PERM = range(LISTS, LISTS + 7)
+T_N, T_OFF = 2 * LISTS, 3 * LISTS
 QROWS = 96
 f32, bf16, i32 = jnp.float32, jnp.bfloat16, jnp.int32
 
@@ -42,8 +45,54 @@
     return i + (i // 2) * 2 + (i // 3) * 2 if group == 0 else i + 2 + i // 2
 
 
-def gather_kernel(q_in, k_in, v_in, order_in, ext_ref, kall, vall, qs, table_out, destt_out,
-                  rx, sorted_, onehot, order_s, key_s, low_s, rank_s, dest_s, destt_s, table_s,
+def fill_tables(n, off, start, ext_row, rep, table, place):
+    lane = iota((CLUSTERS, 128), 1)
+    is_list = lane < LISTS
+    at = jnp.minimum((off >> 4) << 4, LIST - WINDOW)
+    lead = off - at
+    over = jnp.where(is_list & (lead + n > WINDOW), 1, 0)
+    own = is_list & ((lane >> 1) == rep)
+
+    def total(a, hit):
+        return jnp.sum(jnp.where(hit, a, 0).astype(f32), axis=1, keepdims=True).astype(i32)
+
+    off_q, n_q = total(off, own), total(n, own)
+    at_q = jnp.minimum((off_q >> 4) << 4, SPAN - QROWS)
+    windows_q = ((off_q & 15) + n_q + QROWS - 1) // QROWS
+    first = lane < WINDOW
+
+    def both(a, r):
+        return jnp.where(first, a[:, 2 * r:2 * r + 1], a[:, 2 * r + 1:2 * r + 2])
+
+    chosen = jnp.full((CLUSTERS, 128), -1, i32)
+    for r in range(REPS):
+        start_r = both(start, r)
+        spot = lane - jnp.where(first, 0, WINDOW) + start_r - both(lead, r)
+        inside = (spot >= start_r) & (spot < start_r + both(n, r))
+        place[r] = jnp.where(inside, spot, -1)
+        queries = spot - start[:, 2 * r:2 * r + 1] + off_q - at_q
+        chosen = jnp.where(rep == r, jnp.where(inside, queries, -1), chosen)
+    place[REPS] = chosen
+
+    c_row, c_col = iota((CLUSTERS, CLUSTERS), 1), iota((CLUSTERS, CLUSTERS), 0)
+    diagonal = jnp.where(c_row == c_col, 1.0, 0.0).astype(bf16)
+    ext_col = dot_nt(diagonal, jnp.broadcast_to(ext_row, (8, CLUSTERS)).astype(f32).astype(bf16))[:, 0:1].astype(i32)
+    earlier = (ext_col < ext_row) | ((ext_col == ext_row) & (c_col < c_row))
+    rank = jnp.sum(jnp.where(earlier, 1.0, 0.0), axis=0, keepdims=True).astype(i32)
+    perm = jnp.sum(jnp.where(rank == c_col, c_row.astype(f32), 0.0), axis=1, keepdims=True).astype(i32)
+
+    fields = jnp.where(is_list, at + (lane & 1) * LIST, 0)
+    for field, value in ((T_OVER, total(over, is_list)), (T_OFF_Q, off_q), (T_N_Q, n_q), (T_AT_Q, at_q),
+                         (T_OVER_Q, total(over, own)), (T_WINDOWS_Q, windows_q), (T_PERM, perm)):
+        fields = jnp.where(lane == field, value, fields)
+    for j in range(LISTS):
+        fields = jnp.where(lane == T_N + j, n[:, j:j + 1], fields)
+        fields = jnp.where(lane == T_OFF + j, off[:, j:j + 1], fields)
+    table[...] = fields
+
+
+def gather_kernel(q_in, k_in, v_in, order_in, ext_ref, kall, vall, qs, table_out, place_out, destt_out,
+                  rx, sorted_, onehot, order_s, key_s, low_s, rank_s, dest_s, destt_s, table_s, place_s,
                   send_sem, recv_sem, own_sem, order_sem, ysend, yrecv, keep_sem, out_sem):
     me = lax.axis_index("seq")
     rep = lax.axis_index("rep")
@@ -173,20 +222,12 @@
                 listed = listed + product(
                     as_mask((owner == r) & (second == group)), as_mask(cols == r * GROUPS + group))
         pair = as_mask((iota((CLUSTERS, 128), 1) >> 1) == iota((CLUSTERS, 128), 0))
-        counts = product(pair, listed.astype(bf16))
+        counts = product(pair, listed.astype(bf16)).astype(bf16)
         before = as_mask(iota((CLUSTERS, CLUSTERS), 1) < iota((CLUSTERS, CLUSTERS), 0))
-        offsets = product(before, counts.astype(bf16))
-        table_s[0:CLUSTERS, :] = counts.astype(i32)
-        table_s[CLUSTERS:2 * CLUSTERS, :] = offsets.astype(i32)
-        c_row, c_col = iota((CLUSTERS, CLUSTERS), 1), iota((CLUSTERS, CLUSTERS), 0)
-        ext_row = ext_ref[...]
-        ext_col = dot_nt(as_mask(c_row == c_col), jnp.broadcast_to(ext_row, (8, CLUSTERS)).astype(f32).astype(bf16))
-        ext_col = ext_col[:, 0:1].astype(i32)
-        earlier = (ext_row < ext_col) | ((ext_row == ext_col) & (c_row < c_col))
-        place = jnp.sum(jnp.where(earlier, 1.0, 0.0), axis=1, keepdims=True).astype(i32)
-        hit = as_mask(place == iota((CLUSTERS, 128), 1))
-        table_s[2 * CLUSTERS:2 * CLUSTERS + 8, :] = product(
-            iota((8, CLUSTERS), 1).astype(f32).astype(bf16), hit).astype(i32)
+        offsets = product(before, counts)
+        starts = product(counts, upper)
+        fill_tables(counts.astype(f32).astype(i32), offsets.astype(i32), starts.astype(i32), ext_ref[...], rep,
+                    table_s, place_s)
 
     def wait_in(a, group):
         def one(slot, _):
@@ -229,6 +270,7 @@
     per_group = CHUNKS // GROUPS
     table_copy = pltpu.make_async_copy(table_s, table_out, out_sem.at[0])
     destt_copy = pltpu.make_async_copy(destt_s, destt_out, out_sem.at[1])
+    place_copy = pltpu.make_async_copy(place_s, place_out, out_sem.at[2])
     for a in range(3):
         for group in range(GROUPS):
             if a == 0:
@@ -249,6 +291,7 @@
             if a == 0 and group == 0:
                 tables()
                 table_copy.start()
+                place_copy.start()
                 destt_copy.start()
             if a < 2:
                 def forward(i, _):
@@ -261,6 +304,7 @@
                 lax.fori_loop(0, per_group, forward, 0)
 
     table_copy.wait()
+    place_copy.wait()
     destt_copy.wait()
 
     def finish(c, _):
@@ -292,11 +336,12 @@
             jax.ShapeDtypeStruct((REPS, SPAN, DIM), bf16),
             jax.ShapeDtypeStruct((REPS, SPAN, DIM), bf16),
             jax.ShapeDtypeStruct((SPAN, DIM), bf16),
-            jax.ShapeDtypeStruct((2 * CLUSTERS + 8, 128), i32),
+            jax.ShapeDtypeStruct((CLUSTERS, 128), i32),
+            jax.ShapeDtypeStruct((REPS + 1, CLUSTERS, 128), i32),
             jax.ShapeDtypeStruct((LOCAL, HEADS), i32),
         ),
         in_specs=[any_, any_, any_, any_, vmem],
-        out_specs=(any_,) * 5,
+        out_specs=(any_,) * 6,
         scratch_shapes=[
             pltpu.VMEM((3, GROUPS, LIST, DIM), bf16),
             pltpu.VMEM((3, SPAN, DIM), bf16),
@@ -307,7 +352,8 @@
             pltpu.VMEM((4, 128, 128), f32),
             pltpu.VMEM((HEADS, LOCAL), i32),
             pltpu.VMEM((LOCAL, HEADS), i32),
-            pltpu.VMEM((2 * CLUSTERS + 8, 128), i32),
+            pltpu.VMEM((CLUSTERS, 128), i32),
+            pltpu.VMEM((REPS + 1, CLUSTERS, 128), i32),
             pltpu.SemaphoreType.DMA((3, GROUPS, SLOTS)),
             pltpu.SemaphoreType.DMA((3, GROUPS, SLOTS)),
             pltpu.SemaphoreType.DMA((3,)),
@@ -315,7 +361,7 @@
             pltpu.SemaphoreType.DMA((2, 3, CHUNKS)),
             pltpu.SemaphoreType.DMA((2, 3, CHUNKS)),
             pltpu.SemaphoreType.DMA((3, CHUNKS)),
-            pltpu.SemaphoreType.DMA((2,)),
+            pltpu.SemaphoreType.DMA((3,)),
         ],
         compiler_params=pltpu.CompilerParams(
             collective_id=0, has_side_effects=True, vmem_limit_bytes=56 * 2**20),
@@ -326,7 +372,7 @@
 GROUP = 4
 
 
-def attend_kernel(table, list_ref, ext_ref, rep_ref, kall, vall, qs, out, kc, vc, acc):
+def attend_kernel(table, list_ref, ext_ref, rep_ref, place_ref, kall, vall, qs, out, kc, vc, acc):
     ones = jnp.ones((CLUSTER, DIM), bf16)
     rep = rep_ref[0]
 
@@ -334,7 +380,7 @@
         return pl.ds(pl.multiple_of(c * CLUSTER, CLUSTER), CLUSTER)
 
     def extent_of(c, r, group):
-        return table[CLUSTERS + c, r * GROUPS + group], table[c, r * GROUPS + group]
+        return table[c, T_OFF + r * GROUPS + group], table[c, T_N + r * GROUPS + group]
 
     def picked(c, r, k, start):
         lane = iota((1, 128), 1)
@@ -345,7 +391,7 @@
             at = jnp.minimum(lo, LIST - WINDOW)
             first = start + jnp.maximum(lo - off, 0)
             last = start + jnp.minimum(n, lo + WINDOW - off)
-            ats.append(pl.multiple_of(at, 16))
+            ats.append(pl.multiple_of(at + group * LIST, 16))
             shifts.append(start + at - off - group * WINDOW)
             lows.append(first)
             highs.append(last)
@@ -355,17 +401,23 @@
         inside = (place >= jnp.where(is_first, lows[0], lows[1])) & (place < jnp.where(is_first, highs[0], highs[1]))
         return ats, jnp.where(inside, place, -1), start
 
+    def first_windows(c, r):
+        return [pl.multiple_of(table[c, r * GROUPS + g], 16) for g in range(GROUPS)]
+
     def windows_of(ref, ats, r):
-        return [ref[r, pl.ds(ats[g] + g * LIST, WINDOW), :] for g in range(GROUPS)]
-
-    def hot(place, rows, base=0):
-        return jnp.where(iota((rows, 128), 0) + base == place, 1.0, 0.0).astype(bf16)
+        return [ref[r, pl.ds(at, WINDOW), :] for at in ats]
+
+    def hot(place, rows):
+        return jnp.where(iota((rows, 128), 0) == place, 1.0, 0.0).astype(bf16)
 
     def join(c, k):
         start = jnp.int32(0)
         hots, keys, vals = [], [], []
         for r in range(REPS):
-            ats, place, start = picked(c, r, k, start)
+            if k is None:
+                ats, place = first_windows(c, r), place_ref[r, pl.ds(c, 1), :]
+            else:
+                ats, place, start = picked(c, r, k, start)
             hots.append(hot(place, CLUSTER))
             keys += windows_of(kall, ats, r)
             vals += windows_of(vall, ats, r)
@@ -386,12 +438,11 @@
     def compact(i, _):
         cs = [i * GROUP + u for u in range(GROUP)]
         for c in cs:
-            store(c, join(c, 0))
+            store(c, join(c, None))
         for c in cs:
-            most = functools.reduce(jnp.maximum, [rounds(c, r) for r in range(REPS)])
-
-            @pl.when(most > 1)
+            @pl.when(table[c, T_OVER] > 0)
             def _():
+                most = functools.reduce(jnp.maximum, [rounds(c, r) for r in range(REPS)])
                 store(c, lax.fori_loop(0, most, lambda k, whole: whole + join(c, k),
                                        jnp.zeros((CLUSTER, 2 * DIM), f32)))
         return 0
@@ -400,31 +451,33 @@
 
     factor = DIM ** -0.5 * 1.4426950408889634
 
-    def queries_of(c):
-        off0, n0 = extent_of(c, rep, 0)
-        off1, n1 = extent_of(c, rep, 1)
-        return off0 + off1, n0 + n1
-
-    def pick_queries(c, at, off, k):
-        ats, place, _ = picked(c, rep, k, off)
-        rows = [qs[pl.ds(ats[g] + g * LIST, WINDOW), :] for g in range(GROUPS)]
-        return jnp.dot(hot(place, QROWS, at), jnp.concatenate(rows, 0), preferred_element_type=f32)
+    def pick_queries(c, at, k):
+        if k is None:
+            ats, place = first_windows(c, rep), place_ref[REPS, pl.ds(c, 1), :]
+        else:
+            ats, place, _ = picked(c, rep, k, table[c, T_OFF_Q] - at)
+        rows = [qs[pl.ds(a, WINDOW), :] for a in ats]
+        return jnp.dot(hot(place, QROWS), jnp.concatenate(rows, 0), preferred_element_type=f32)
 
     def attend_rows(cs, k, size, slow):
         rows, live, blocks, tops, scores, queries = [], [], [], [], [], []
         for c in cs:
-            off, n = queries_of(c)
-            lo = (off // 16) * 16 + k * QROWS
-            at = jnp.minimum(lo, SPAN - QROWS)
+            off, n = table[c, T_OFF_Q], table[c, T_N_Q]
+            if slow:
+                lo = (off // 16) * 16 + k * QROWS
+                at = jnp.minimum(lo, SPAN - QROWS)
+            else:
+                lo, at = 0, table[c, T_AT_Q]
             rows.append(pl.ds(pl.multiple_of(at, 16), QROWS))
             row = iota((QROWS, DIM), 0) + at
-            live.append((row >= jnp.maximum(off, lo)) & (row < jnp.minimum(off + n, lo + QROWS)))
-            blocks.append([span(list_ref[c, jnp.where(j < ext_ref[c], j, 0)]) for j in range(size)])
+            live.append((row >= jnp.maximum(off, lo)) & (row < jnp.minimum(off + n, lo + QROWS)) if slow
+                        else (row >= off) & (row < off + n))
+            blocks.append([span(list_ref[jnp.where(j < ext_ref[c], j, 0), c]) for j in range(size)])
             if slow:
-                query = lax.fori_loop(0, rounds(c, rep), lambda i, q: q + pick_queries(c, at, off, i),
+                query = lax.fori_loop(0, rounds(c, rep), lambda i, q: q + pick_queries(c, at, i),
                                       jnp.zeros((QROWS, DIM), f32))
             else:
-                query = pick_queries(c, at, off, 0)
+                query = pick_queries(c, at, None)
             queries.append(query.astype(bf16))
         for u in range(len(cs)):
             scores.append([dot_nt(queries[u], kc[b, :]) for b in blocks[u]])
@@ -443,20 +496,18 @@
             acc[rows[u], :] = jnp.where(live[u], results[u], acc[rows[u], :])
 
     def attend(g, _):
-        cs = [table[2 * CLUSTERS, g * GROUP + u] for u in range(GROUP)]
+        cs = [table[g * GROUP + u, T_PERM] for u in range(GROUP)]
         size_most = ext_ref[cs[-1]]
         for size in range(1, 9):
             @pl.when(size_most == size)
             def _():
                 attend_rows(cs, 0, size, False)
         for c in cs:
-            off, n = queries_of(c)
-
             def more(k, _):
                 attend_rows([c], k, 8, True)
                 return 0
 
-            lax.fori_loop(jnp.where(rounds(c, rep) > 1, 0, 1), (off % 16 + n + QROWS - 1) // QROWS, more, 0)
+            lax.fori_loop(jnp.where(table[c, T_OVER_Q] > 0, 0, 1), table[c, T_WINDOWS_Q], more, 0)
         return 0
 
     lax.fori_loop(0, CLUSTERS // GROUP, attend, 0)
@@ -469,13 +520,13 @@
     lax.fori_loop(0, SPAN // 512, finish, 0)
 
 
-def attend_call(table, listed, ext, rep, kall, vall, qs):
+def attend_call(table, listed, ext, rep, place, kall, vall, qs):
     smem = pl.BlockSpec(memory_space=pltpu.SMEM)
     vmem = pl.BlockSpec(memory_space=pltpu.VMEM)
     return pl.pallas_call(
         attend_kernel,
         out_shape=jax.ShapeDtypeStruct((SPAN, DIM), bf16),
-        in_specs=[smem] * 4 + [vmem] * 3,
+        in_specs=[smem] * 4 + [vmem] * 4,
         out_specs=vmem,
         scratch_shapes=[
             pltpu.VMEM((TOKENS, DIM), bf16),
@@ -484,17 +535,21 @@
         ],
         compiler_params=pltpu.CompilerParams(vmem_limit_bytes=56 * 2**20),
         name="attend",
-    )(table, listed, ext, rep, kall, vall, qs)
+    )(table, listed, ext, rep, place, kall, vall, qs)
 
 
 HALF = HEADS // 2
 
 
-def return_kernel(mixed, destt_ref, out, partner_s, both_s, onehot, tx, swap_send, swap_recv,
-                  send_sem, recv_sem, own_sem):
+def return_kernel(mixed_in, destt_in, out, mixed, destt_ref, partner_s, both_s, onehot, tx, swap_send, swap_recv,
+                  send_sem, recv_sem, own_sem, in_sem):
     guide, me = lax.axis_index("guide"), lax.axis_index("seq")
     other = 1 - guide
     head_guide, head_col = me // HALF, me % HALF
+    mixed_copy = pltpu.make_async_copy(mixed_in, mixed, in_sem.at[0])
+    destt_copy = pltpu.make_async_copy(destt_in, destt_ref, in_sem.at[1])
+    mixed_copy.start()
+    destt_copy.start()
 
     barrier = pltpu.get_barrier_semaphore()
     pl.semaphore_signal(barrier, inc=1, device_id={"guide": other}, device_id_type=MESH)
@@ -517,16 +572,18 @@
         pl.semaphore_wait(barrier, HALF)
 
     swap = pltpu.make_async_remote_copy(
-        src_ref=mixed, dst_ref=partner_s, send_sem=swap_send, recv_sem=swap_recv,
+        src_ref=mixed_in, dst_ref=partner_s, send_sem=swap_send, recv_sem=swap_recv,
         device_id={"guide": other}, device_id_type=MESH)
     swap.start()
 
+    destt_copy.wait()
     destt = destt_ref[...]
     picked = jnp.where(guide == 0, destt[:, :HALF], destt[:, HALF:])
     for i in range(HALF):
         for c in range(SPAN // 512):
             onehot[i * LOCAL:(i + 1) * LOCAL, c * 512:(c + 1) * 512] = jnp.where(
                 picked[:, i:i + 1] == iota((LOCAL, 512), 1) + c * 512, 1.0, 0.0).astype(bf16)
+    mixed_copy.wait()
     swap.wait()
 
     def combine(c, _):
@@ -596,13 +653,15 @@
 
 
 def return_call(mixed, destt):
-    vmem = pl.BlockSpec(memory_space=pltpu.VMEM)
+    any_ = pl.BlockSpec(memory_space=pl.ANY)
     return pl.pallas_call(
         return_kernel,
         out_shape=jax.ShapeDtypeStruct((LOCAL, HALF * DIM), bf16),
-        in_specs=[vmem, vmem],
-        out_specs=pl.BlockSpec(memory_space=pl.ANY),
+        in_specs=[any_, any_],
+        out_specs=any_,
         scratch_shapes=[
+            pltpu.VMEM((SPAN, DIM), bf16),
+            pltpu.VMEM((LOCAL, HEADS), i32),
             pltpu.VMEM((SPAN, DIM), bf16),
             pltpu.VMEM((SPAN, DIM), bf16),
             pltpu.VMEM((SPAN // 2, SPAN), bf16),
@@ -612,6 +671,7 @@
             pltpu.SemaphoreType.DMA((HALF,)),
             pltpu.SemaphoreType.DMA((HALF,)),
             pltpu.SemaphoreType.DMA,
+            pltpu.SemaphoreType.DMA((2,)),
         ],
         compiler_params=pltpu.CompilerParams(
             collective_id=1, has_side_effects=True, vmem_limit_bytes=48 * 2**20),
@@ -620,10 +680,10 @@
 
 
 def on_device(queries, key_vectors, value_vectors, cluster_order, key_blocks, extents):
-    kall, vall, qs, table, destt = gather_call(
+    kall, vall, qs, table, place, destt = gather_call(
         queries[0], key_vectors[0], value_vectors[0], cluster_order, extents)
     rep = lax.axis_index("rep").astype(i32).reshape(1)
-    mixed = attend_call(table, key_blocks[0], extents[0], rep, kall, vall, qs)
+    mixed = attend_call(table, key_blocks[0].T, extents[0], rep, place, kall, vall, qs)
     return return_call(mixed, destt)
 
 

time: 173 us -> 164 us (0.948)
  Pallas kernels: 170 us -> 162 us
    pallas_call x1, Pallas kernels: 34 us -> 24.2 us  [attend_call(): pl.pallas_call(attend_kernel, out_shape=jax.ShapeDtypeStruct((SPAN, DIM),...]
    pallas_call x1, Pallas kernels: 34.8 us -> 37 us  [return_call(): pl.pallas_call(return_kernel, out_shape=jax.ShapeDtypeStruct((LOCAL, HALF...]
where the time goes in v4:
time: 164 us
  Pallas kernels  162 us (99%)
  local copies, waits for them, and re-layouts  2.02 us (1%)
    pallas_call x1, Pallas kernels, gather_call(): pl.pallas_call(gather_kernel, out_shape=(jax.ShapeDtypeStruct((REPS, SPAN...  101 us
    pallas_call x1, Pallas kernels, return_call(): pl.pallas_call(return_kernel, out_shape=jax.ShapeDtypeStruct((LOCAL, HALF...  37 us
    pallas_call x1, Pallas kernels, attend_call(): pl.pallas_call(attend_kernel, out_shape=jax.ShapeDtypeStruct((SPAN, DIM),...  24.2 us

profile of v4, /device:TPU:6, one launch (start us, length us, event | category | flops | bytes accessed | tf_op | source)
XLA Modules:
  0.0 164.0 jit_solution(3454263092185819254)
XLA Ops:
  0.0 100.8 %gather_sorted.1 = (bf16[4,4096,128]{2,1,0:T(8,128)(2,1)}, bf16[4,4096,128]{2,1,0:T(8,128)(2,1)}, bf16[4096,128]{1,0:T(8,128)(2,1)}, s32[64,128]{1,0:T(8,128)}, ...) custom-call(bf16[128,4096]{1,0:T(8,128)(2,1)} %bitcast.8, bf16[128,4096]{1,0:T(8,128)(2,1)} %bitcast.9, ...), custom_call_target="tpu_custom_call" | custom-call | tf_op jit(solution)/shard_map/gather_sorted/pallas_call | solution.py:333
  100.8 0.0 copy-start.1
  100.8 24.2 %attend.1.mixed_in = bf16[4096,128]{1,0:T(8,128)(2,1)} custom-call(s32[64,128]{1,0:T(8,128)} %get-tuple-element.11.table, s32[8,64]{1,0:T(8,128)} %bitcast.11, s32[64]{0:T(128)} %bitcast.12, s32[1]{0:T(128)} %bitcast.6.rep_ref, s32[5,64,128]{2,1,0:T(8,128)} %get-tuple-element.12.place_ref, bf16[4,4096,128]{2,1,0:T(8,128)(2,1)} %get-tuple-element.13.kall, ...), custom_call_target="tpu_custom_call" | custom-call | tf_op jit(solution)/shard_map/attend/pallas_call | solution.py:526
  125.0 0.0 copy-done.1
  125.0 0.0 copy-start
  125.0 1.2 copy-done
  126.3 37.0 %return_tokens.1 = bf16[128,2048]{1,0:T(8,128)(2,1)S(1)} custom-call(bf16[4096,128]{1,0:T(8,128)(2,1)S(1)} %copy-done, s32[128,32]{1,0:T(8,128)S(1)} %copy-done.1), custom_call_target="tpu_custom_call" | custom-call | tf_op jit(solution)/shard_map/return_tokens/pallas_call | solution.py:657
  163.2 0.8 copy.8
Async XLA Ops:
  100.8 24.2 %copy-start.1 = (s32[128,32]{1,0:T(8,128)S(1)}, s32[128,32]{1,0:T(8,128)}, u32[]{:S(2)}) copy-start(s32[128,32]{1,0:T(8,128)} %get-tuple-element.16.destt_in) | copy-start | bytes 49156
  125.0 1.2 copy-start

commit v5 on v4

--- a/solution.py
+++ b/solution.py
@@ -41,8 +41,11 @@
     return lax.broadcasted_iota(i32, shape, dim)
 
 
-def z_distance(group, i):
-    return i + (i // 2) * 2 + (i // 3) * 2 if group == 0 else i + 2 + i // 2
+def z_distance(group, dx, i):
+    far = 4 * (dx // 2)
+    if group == 0:
+        return i + (i // 2) * 5 + (i // 3) * (far - 6)
+    return i + 2 + (1 - (i + 2) // 3) * (4 - far)
 
 
 def fill_tables(n, off, start, ext_row, rep, table, place):
@@ -102,7 +105,8 @@
     alls = (kall, vall)
 
     def at_distance(group, slot, sign):
-        dx, dz = slot // 4, z_distance(group, slot % 4)
+        dx = slot // 4
+        dz = z_distance(group, dx, slot % 4)
         return lax.rem(x + sign * dx + SEQ_X, SEQ_X) * SEQ_Z + lax.rem(z + sign * dz + SEQ_Z, SEQ_Z)
 
     def order_copy(u):
@@ -138,14 +142,16 @@
         return pltpu.make_async_copy(
             ins[a].at[:, pl.ds(pl.multiple_of(me * DIM, DIM), DIM)], rx.at[a, 0, pl.ds(0, LOCAL)], own_sem.at[a])
 
-    for a in range(3):
-        own_copy(a).start()
-        for group in range(GROUPS):
-            def send(slot, _):
-                a2a_copy(a, group, slot).start()
-                return 0
-
-            lax.fori_loop(1 - group, SLOTS, send, 0)
+    units = ((0, 0), (1, 0), (0, 1), (1, 1), (2, 0), (2, 1))
+    for a, group in units:
+        if group == 0:
+            own_copy(a).start()
+
+        def send(slot, _):
+            a2a_copy(a, group, slot).start()
+            return 0
+
+        lax.fori_loop(1 - group, SLOTS, send, 0)
 
     def fetched(u, _):
         order_copy(u).wait()
@@ -156,8 +162,10 @@
     order = order_s[...]
     block = order >> 7
     owner = block & (REPS - 1)
-    away = (z - (block >> 2)) & (SEQ_Z - 1)
-    second = jnp.where((away == 0) | (away == 1) | (away == 4) | (away == 7), 0, 1)
+    away_x = (x - (block >> 5)) & (SEQ_X - 1)
+    away_z = (z - (block >> 2)) & (SEQ_Z - 1)
+    near = (away_z == 0) | (away_z == 1) | (away_z == 7) | (away_z == 2 + 4 * (away_x >> 1))
+    second = jnp.where(near, 0, 1)
     mine = owner == rep
     rows, cols = iota((128, 128), 0), iota((128, 128), 1)
     as_mask = lambda hit: jnp.where(hit, 1.0, 0.0).astype(bf16)
@@ -271,37 +279,36 @@
     table_copy = pltpu.make_async_copy(table_s, table_out, out_sem.at[0])
     destt_copy = pltpu.make_async_copy(destt_s, destt_out, out_sem.at[1])
     place_copy = pltpu.make_async_copy(place_s, place_out, out_sem.at[2])
-    for a in range(3):
-        for group in range(GROUPS):
-            if a == 0:
-                build(group)
-            wait_in(a, group)
-
-            def sort(i, _):
+    for a, group in units:
+        if a == 0:
+            build(group)
+        wait_in(a, group)
+
+        def sort(i, _):
+            c = group * per_group + i
+            sorted_[a, rows_of(c)] = jnp.dot(
+                onehot[group, rows_of(i), :], rx[a, group], preferred_element_type=f32).astype(bf16)
+            if a < 2:
+                ycopy(a, 0, c).start()
+                ycopy(a, 1, c).start()
+            keep_copy(a, c).start()
+            return 0
+
+        lax.fori_loop(0, per_group, sort, 0)
+        if a == 0 and group == 0:
+            tables()
+            table_copy.start()
+            place_copy.start()
+            destt_copy.start()
+        if a < 2:
+            def forward(i, _):
                 c = group * per_group + i
-                sorted_[a, rows_of(c)] = jnp.dot(
-                    onehot[group, rows_of(i), :], rx[a, group], preferred_element_type=f32).astype(bf16)
-                if a < 2:
-                    ycopy(a, 0, c).start()
-                    ycopy(a, 1, c).start()
-                keep_copy(a, c).start()
+                wait_y(a, 0, c)
+                wait_y(a, 1, c)
+                ycopy(a, 2, c).start()
                 return 0
 
-            lax.fori_loop(0, per_group, sort, 0)
-            if a == 0 and group == 0:
-                tables()
-                table_copy.start()
-                place_copy.start()
-                destt_copy.start()
-            if a < 2:
-                def forward(i, _):
-                    c = group * per_group + i
-                    wait_y(a, 0, c)
-                    wait_y(a, 1, c)
-                    ycopy(a, 2, c).start()
-                    return 0
-
-                lax.fori_loop(0, per_group, forward, 0)
+            lax.fori_loop(0, per_group, forward, 0)
 
     table_copy.wait()
     place_copy.wait()
@@ -369,15 +376,17 @@
     )(q, k, v, order, ext)
 
 
-GROUP = 4
+GROUP = 8
 
 
 def attend_kernel(table, list_ref, ext_ref, rep_ref, place_ref, kall, vall, qs, out, kc, vc, acc):
-    ones = jnp.ones((CLUSTER, DIM), bf16)
     rep = rep_ref[0]
 
     def span(c):
         return pl.ds(pl.multiple_of(c * CLUSTER, CLUSTER), CLUSTER)
+
+    def half_span(c):
+        return pl.ds(pl.multiple_of(c * DIM, DIM), DIM)
 
     def extent_of(c, r, group):
         return table[c, T_OFF + r * GROUPS + group], table[c, T_N + r * GROUPS + group]
@@ -425,8 +434,8 @@
         return jnp.dot(jnp.concatenate(hots, 1), kv, preferred_element_type=f32)
 
     def store(c, whole):
-        kc[span(c), :] = whole[:, :DIM].astype(bf16)
-        vc[span(c), :] = jnp.concatenate([whole[:, DIM:].astype(bf16), ones], 1)
+        kc[half_span(c), :] = whole[:, :DIM].T.astype(bf16)
+        vc[span(c), :] = whole[:, DIM:].astype(bf16)
 
     def rounds(c, r):
         most = jnp.int32(0)
@@ -472,7 +481,7 @@
             row = iota((QROWS, DIM), 0) + at
             live.append((row >= jnp.maximum(off, lo)) & (row < jnp.minimum(off + n, lo + QROWS)) if slow
                         else (row >= off) & (row < off + n))
-            blocks.append([span(list_ref[jnp.where(j < ext_ref[c], j, 0), c]) for j in range(size)])
+            blocks.append([list_ref[jnp.where(j < ext_ref[c], j, 0), c] for j in range(size)])
             if slow:
                 query = lax.fori_loop(0, rounds(c, rep), lambda i, q: q + pick_queries(c, at, i),
                                       jnp.zeros((QROWS, DIM), f32))
@@ -480,18 +489,20 @@
                 query = pick_queries(c, at, None)
             queries.append(query.astype(bf16))
         for u in range(len(cs)):
-            scores.append([dot_nt(queries[u], kc[b, :]) for b in blocks[u]])
+            scores.append([jnp.dot(queries[u], kc[half_span(b), :], preferred_element_type=f32) for b in blocks[u]])
         for u in range(len(cs)):
             tops.append(jnp.max(functools.reduce(jnp.maximum, scores[u]), axis=1, keepdims=True))
         results = []
         for u, c in enumerate(cs):
-            mixed = None
+            powers, sums = [], None
             for j in range(size):
                 top = tops[u] if j == 0 else jnp.where(j < ext_ref[c], tops[u], jnp.inf)
-                power = jnp.exp2((scores[u][j] - top) * factor).astype(bf16)
-                part = jnp.dot(power, vc[blocks[u][j], :], preferred_element_type=f32)
-                mixed = part if mixed is None else mixed + part
-            results.append(mixed[:, :DIM] / mixed[:, DIM:])
+                power = jnp.exp2((scores[u][j] - top) * factor)
+                sums = power if sums is None else sums + power
+                powers.append(power.astype(bf16))
+            mixed = jnp.dot(jnp.concatenate(powers, 1), jnp.concatenate([vc[span(b), :] for b in blocks[u]], 0),
+                            preferred_element_type=f32)
+            results.append(mixed / jnp.sum(sums, axis=1, keepdims=True))
         for u in range(len(cs)):
             acc[rows[u], :] = jnp.where(live[u], results[u], acc[rows[u], :])
 
@@ -529,8 +540,8 @@
         in_specs=[smem] * 4 + [vmem] * 4,
         out_specs=vmem,
         scratch_shapes=[
+            pltpu.VMEM((CLUSTERS * DIM, CLUSTER), bf16),
             pltpu.VMEM((TOKENS, DIM), bf16),
-            pltpu.VMEM((TOKENS, 2 * DIM), bf16),
             pltpu.VMEM((SPAN, DIM), f32),
         ],
         compiler_params=pltpu.CompilerParams(vmem_limit_bytes=56 * 2**20),
@@ -674,7 +685,7 @@
             pltpu.SemaphoreType.DMA((2,)),
         ],
         compiler_params=pltpu.CompilerParams(
-            collective_id=1, has_side_effects=True, vmem_limit_bytes=48 * 2**20),
+            collective_id=1, has_side_effects=True, vmem_limit_bytes=60 * 2**20),
         name="return_tokens",
     )(mixed, destt)
 

time: 164 us -> 154 us (0.939)
  Pallas kernels: 162 us -> 152 us
    pallas_call x1, Pallas kernels: 37 us -> 23.5 us  [return_call(): pl.pallas_call(return_kernel, out_shape=jax.ShapeDtypeStruct((LOCAL, HALF...]
    pallas_call x1, Pallas kernels: 24.2 us -> 28.4 us  [attend_call(): pl.pallas_call(attend_kernel, out_shape=jax.ShapeDtypeStruct((SPAN, DIM),...]
where the time goes in v5:
time: 154 us
  Pallas kernels  152 us (99%)
  local copies, waits for them, and re-layouts  1.88 us (1%)
    pallas_call x1, Pallas kernels, gather_call(): pl.pallas_call(gather_kernel, out_shape=(jax.ShapeDtypeStruct((REPS, SPAN...  101 us
    pallas_call x1, Pallas kernels, attend_call(): pl.pallas_call(attend_kernel, out_shape=jax.ShapeDtypeStruct((SPAN, DIM),...  28.4 us
    pallas_call x1, Pallas kernels, return_call(): pl.pallas_call(return_kernel, out_shape=jax.ShapeDtypeStruct((LOCAL, HALF...  23.5 us

profile of v5, /device:TPU:6, one launch (start us, length us, event | category | flops | bytes accessed | tf_op | source)
XLA Modules:
  0.0 154.3 jit_solution(8959160295280614294)
XLA Ops:
  0.0 100.5 %gather_sorted.1 = (bf16[4,4096,128]{2,1,0:T(8,128)(2,1)}, bf16[4,4096,128]{2,1,0:T(8,128)(2,1)}, bf16[4096,128]{1,0:T(8,128)(2,1)}, s32[64,128]{1,0:T(8,128)}, ...) custom-call(bf16[128,4096]{1,0:T(8,128)(2,1)} %bitcast.8, bf16[128,4096]{1,0:T(8,128)(2,1)} %bitcast.9, ...), custom_call_target="tpu_custom_call" | custom-call | tf_op jit(solution)/shard_map/gather_sorted/pallas_call | solution.py:340
  100.5 28.4 %attend.1.mixed_in = bf16[4096,128]{1,0:T(8,128)(2,1)} custom-call(s32[64,128]{1,0:T(8,128)} %get-tuple-element.11.table, s32[8,64]{1,0:T(8,128)} %bitcast.11, s32[64]{0:T(128)} %bitcast.12, s32[1]{0:T(128)} %bitcast.6.rep_ref, s32[5,64,128]{2,1,0:T(8,128)} %get-tuple-element.12.place_ref, bf16[4,4096,128]{2,1,0:T(8,128)(2,1)} %get-tuple-element.13.kall, ...), custom_call_target="tpu_custom_call" | custom-call | tf_op jit(solution)/shard_map/attend/pallas_call | solution.py:537
  128.9 23.5 %return_tokens.1 = bf16[128,2048]{1,0:T(8,128)(2,1)} custom-call(bf16[4096,128]{1,0:T(8,128)(2,1)} %attend.1.mixed_in, s32[128,32]{1,0:T(8,128)} %get-tuple-element.16.destt_in), custom_call_target="tpu_custom_call" | custom-call | tf_op jit(solution)/shard_map/return_tokens/pallas_call | solution.py:668
  152.4 1.9 %copy.8 = bf16[128,2048]{1,0:T(8,128)(2,1)} copy(bf16[128,2048]{1,0:T(8,128)(2,1)} %return_tokens.1) | data formatting | bytes 1048576

commit v6 on v5

--- a/solution.py
+++ b/solution.py
@@ -19,7 +19,6 @@
 LOCAL = 128
 CLUSTERS = TOKENS // CLUSTER
 CHUNK = 512
-CHUNKS = SPAN // CHUNK
 GROUPS = 2
 SLOTS = HEADS // GROUPS
 LIST = SPAN // GROUPS
@@ -95,14 +94,14 @@
 
 
 def gather_kernel(q_in, k_in, v_in, order_in, ext_ref, kall, vall, qs, table_out, place_out, destt_out,
-                  rx, sorted_, onehot, order_s, key_s, low_s, rank_s, dest_s, destt_s, table_s, place_s,
+                  raw, raw_q, staged, staged_q, order_s, key_s, low_s, rank_s, dest_s, destt_s, table_s, place_s,
                   send_sem, recv_sem, own_sem, order_sem, ysend, yrecv, keep_sem, out_sem):
     me = lax.axis_index("seq")
     rep = lax.axis_index("rep")
     x, z = me // SEQ_Z, me % SEQ_Z
     right, left = lax.rem(rep + 1, REPS), lax.rem(rep + REPS - 1, REPS)
+    far = lax.rem(rep + 2, REPS)
     ins = (k_in, v_in, q_in)
-    alls = (kall, vall)
 
     def at_distance(group, slot, sign):
         dx = slot // 4
@@ -130,17 +129,21 @@
     pl.semaphore_signal(barrier, inc=1, device_id={"rep": left}, device_id_type=MESH)
     pl.semaphore_wait(barrier, HEADS - 1 + 2)
 
+    def landing(a, group, slot):
+        rows = pl.ds(pl.multiple_of(slot * LOCAL, LOCAL), LOCAL)
+        return raw.at[a, rep, group, rows] if a < 2 else raw_q.at[group, rows]
+
     def a2a_copy(a, group, slot):
         peer = at_distance(group, slot, 1)
         return pltpu.make_async_remote_copy(
             src_ref=ins[a].at[:, pl.ds(pl.multiple_of(peer * DIM, DIM), DIM)],
-            dst_ref=rx.at[a, group, pl.ds(pl.multiple_of(slot * LOCAL, LOCAL), LOCAL)],
+            dst_ref=landing(a, group, slot),
             send_sem=send_sem.at[a, group, slot], recv_sem=recv_sem.at[a, group, slot],
             device_id={"seq": peer}, device_id_type=MESH)
 
     def own_copy(a):
         return pltpu.make_async_copy(
-            ins[a].at[:, pl.ds(pl.multiple_of(me * DIM, DIM), DIM)], rx.at[a, 0, pl.ds(0, LOCAL)], own_sem.at[a])
+            ins[a].at[:, pl.ds(pl.multiple_of(me * DIM, DIM), DIM)], landing(a, 0, 0), own_sem.at[a])
 
     units = ((0, 0), (1, 0), (0, 1), (1, 1), (2, 0), (2, 1))
     for a, group in units:
@@ -152,6 +155,71 @@
             return 0
 
         lax.fori_loop(1 - group, SLOTS, send, 0)
+
+    def rows_of(c):
+        return pl.ds(pl.multiple_of(c * CHUNK, CHUNK), CHUNK)
+
+    def ycopy(a, kind, group, c):
+        if kind == 0:
+            slot, to = rep, right
+        elif kind == 1:
+            slot, to = rep, left
+        else:
+            even = lax.rem(c, 2) == 0
+            slot = jnp.where(even, left, right)
+            to = jnp.where(even, right, left)
+        piece = raw.at[a, slot, group, rows_of(c)]
+        return pltpu.make_async_remote_copy(
+            src_ref=piece, dst_ref=piece,
+            send_sem=ysend.at[a, kind, group, c], recv_sem=yrecv.at[a, kind, group, c],
+            device_id={"rep": to}, device_id_type=MESH)
+
+    def wait_y(a, kind, group, c):
+        piece = raw.at[a, (left, right, far)[kind], group, rows_of(c)]
+        pltpu.make_async_remote_copy(
+            src_ref=piece, dst_ref=piece,
+            send_sem=ysend.at[a, kind, group, c], recv_sem=yrecv.at[a, kind, group, c],
+            device_id={"rep": right}, device_id_type=MESH).wait_recv()
+
+    def wait_slot(a, group, slot, _):
+        a2a_copy(a, group, slot).wait_recv()
+        return 0
+
+    per_chunk, chunks = CHUNK // LOCAL, LIST // CHUNK
+
+    def pass_on(a, group):
+        def one(c, _):
+            ycopy(a, 0, group, c).start()
+            ycopy(a, 1, group, c).start()
+            return 0
+
+        def arrived(c, _):
+            lax.fori_loop(0, per_chunk, lambda i, _: wait_slot(a, group, c * per_chunk + i, _), 0)
+            return one(c, _)
+
+        if group == 0:
+            lax.fori_loop(1, per_chunk, lambda i, _: wait_slot(a, group, i, _), 0)
+            own_copy(a).wait()
+            one(0, 0)
+        lax.fori_loop(1 - group, chunks, arrived, 0)
+
+    def forward(a, group):
+        def one(c, _):
+            wait_y(a, 0, group, c)
+            wait_y(a, 1, group, c)
+            ycopy(a, 2, group, c).start()
+            return 0
+
+        lax.fori_loop(0, chunks, one, 0)
+
+    def settle(a, group):
+        def one(c, _):
+            wait_y(a, 2, group, c)
+            return 0
+
+        lax.fori_loop(0, chunks, one, 0)
+
+    pass_on(0, 0)
 
     def fetched(u, _):
         order_copy(u).wait()
@@ -173,17 +241,18 @@
     upper, lower = as_mask(rows < cols), as_mask(cols < rows)
     to_cluster, past_cluster = as_mask(cols < (rows >> 1) * 2), as_mask(cols < (rows >> 1) * 2 + 2)
     ones = jnp.ones((128, 128), bf16)
-    ranks, befores, pasts = [], [], []
-    for group in range(GROUPS):
-        present = as_mask(mine & (second == group))
-        totals = product(present, ones).astype(bf16)
-        ranks.append(product(present, upper) + product(lower, totals))
-        befores.append(product(to_cluster, totals))
-        pasts.append(product(past_cluster, totals))
-    rank = jnp.where(second == 0, ranks[0], ranks[1])
-    whole = jnp.where(second == 0, ranks[0] + befores[1], ranks[1] + pasts[0])
+    rank = jnp.zeros((128, 128), f32)
+    for r in range(REPS):
+        for group in range(GROUPS):
+            hit = (owner == r) & (second == group)
+            present = as_mask(hit)
+            totals = product(present, ones).astype(bf16)
+            rank = jnp.where(hit, product(present, upper) + product(lower, totals), rank)
+    own_totals = [product(as_mask(mine & (second == group)), ones).astype(bf16) for group in range(GROUPS)]
+    whole = rank + jnp.where(second == 0, product(to_cluster, own_totals[1]), product(past_cluster, own_totals[0]))
     rank_hi, whole_hi = jnp.floor(rank * (1.0 / 64.0)), jnp.floor(whole * (1.0 / 64.0))
-    key_s[...] = jnp.where(mine, block >> 2, -1)
+    key_s[0] = block
+    key_s[1] = jnp.where(mine, block >> 2, -1)
     low_s[...] = order & (LOCAL - 1)
     rank_s[0] = rank_hi
     rank_s[1] = rank - 64.0 * rank_hi
@@ -194,34 +263,24 @@
         d, dt = carry
         parts, bs = [[], [], [], []], []
         base = pl.multiple_of(step * 32, 32)
-        key8, low8 = key_s[pl.ds(base, 32), :], low_s[pl.ds(base, 32), :]
-        rank8 = [rank_s[i, pl.ds(base, 32), :] for i in range(4)]
+        keys = [key_s[i, pl.ds(base, 32), :] for i in range(2)]
+        low = low_s[pl.ds(base, 32), :]
+        values = [rank_s[i, pl.ds(base, 32), :] for i in range(4)]
         for j in range(32):
-            hit = iota((HEADS, 128), 0) == key8[j:j + 1]
+            hit_all = iota((128, 128), 0) == keys[0][j:j + 1]
+            hit_own = iota((HEADS, 128), 0) == keys[1][j:j + 1]
             for i in range(4):
-                parts[i].append(jnp.where(hit, rank8[i][j:j + 1], 0.0).astype(bf16))
-            bs.append(as_mask(iota((128, 128), 0) == low8[j:j + 1]))
+                parts[i].append(jnp.where(hit_all if i < 2 else hit_own, values[i][j:j + 1], 0.0).astype(bf16))
+            bs.append(as_mask(iota((128, 128), 0) == low[j:j + 1]))
         parts = [jnp.concatenate(p, 1) for p in parts]
         right_m = jnp.concatenate(bs, 1)
         d = d + dot_nt(jnp.concatenate(parts[:2], 0), right_m)
         dt = dt + dot_nt(right_m, jnp.concatenate(parts[2:], 0))
         return d, dt
 
-    d, dt = lax.fori_loop(0, 4, accumulate, (jnp.zeros((2 * HEADS, 128), f32), jnp.zeros((128, 2 * HEADS), f32)))
-    dest_s[...] = (64.0 * d[:HEADS] + d[HEADS:]).astype(i32)
+    d, dt = lax.fori_loop(0, 4, accumulate, (jnp.zeros((256, 128), f32), jnp.zeros((128, 2 * HEADS), f32)))
+    dest_s[...] = (64.0 * d[:128] + d[128:]).astype(i32)
     destt_s[...] = (64.0 * dt[:, :HEADS] + dt[:, HEADS:]).astype(i32)
-
-    def build(group):
-        for slot in range(SLOTS):
-            row = dest_s[pl.ds(at_distance(group, slot, -1), 1), :]
-
-            def block_of(kb, _):
-                base = pl.multiple_of(kb * 256, 256)
-                onehot[group, pl.ds(base, 256), slot * 128:(slot + 1) * 128] = as_mask(
-                    iota((256, 128), 0) + base == row)
-                return 0
-
-            lax.fori_loop(0, LIST // 256, block_of, 0)
 
     def tables():
         listed = jnp.zeros((128, 128), f32)
@@ -237,96 +296,81 @@
         fill_tables(counts.astype(f32).astype(i32), offsets.astype(i32), starts.astype(i32), ext_ref[...], rep,
                     table_s, place_s)
 
-    def wait_in(a, group):
-        def one(slot, _):
-            a2a_copy(a, group, slot).wait_recv()
+    def sort(r, group, is_query):
+        lines = [dest_s[pl.ds(at_distance(group, slot, -1) * REPS + r, 1), :] for slot in range(SLOTS)]
+
+        def some(c, _):
+            base = pl.multiple_of(c * CHUNK, CHUNK)
+            hot = jnp.concatenate([as_mask(iota((CHUNK, 128), 0) + base == line) for line in lines], 1)
+            rows = pl.ds(pl.multiple_of(group * LIST + base, CHUNK), CHUNK)
+            if is_query:
+                staged_q[rows, :] = product(hot, raw_q[group]).astype(bf16)
+            else:
+                both = product(hot, jnp.concatenate([raw[0, r, group], raw[1, r, group]], 1)).astype(bf16)
+                staged[0, r, rows, :] = both[:, :DIM]
+                staged[1, r, rows, :] = both[:, DIM:]
             return 0
 
-        lax.fori_loop(1 - group, SLOTS, one, 0)
-        if group == 0:
-            own_copy(a).wait()
-
-    def rows_of(c):
-        return pl.ds(pl.multiple_of(c * CHUNK, CHUNK), CHUNK)
-
-    def ycopy(a, kind, c):
-        if kind == 0:
-            src, slot, to = sorted_.at[a, rows_of(c)], rep, right
-        elif kind == 1:
-            src, slot, to = sorted_.at[a, rows_of(c)], rep, left
-        else:
-            even = lax.rem(c, 2) == 0
-            slot = jnp.where(even, left, right)
-            to = jnp.where(even, right, left)
-            src = alls[a].at[slot, rows_of(c)]
-        return pltpu.make_async_remote_copy(
-            src_ref=src, dst_ref=alls[a].at[slot, rows_of(c)],
-            send_sem=ysend.at[a, kind, c], recv_sem=yrecv.at[a, kind, c],
-            device_id={"rep": to}, device_id_type=MESH)
-
-    def keep_copy(a, c):
-        to = alls[a].at[rep, rows_of(c)] if a < 2 else qs.at[rows_of(c)]
-        return pltpu.make_async_copy(sorted_.at[a, rows_of(c)], to, keep_sem.at[a, c])
-
-    def wait_y(a, kind, c):
-        slot = (left, right, lax.rem(rep + 2, REPS))[kind]
-        pltpu.make_async_remote_copy(
-            src_ref=sorted_.at[a, rows_of(c)], dst_ref=alls[a].at[slot, rows_of(c)],
-            send_sem=ysend.at[a, kind, c], recv_sem=yrecv.at[a, kind, c],
-            device_id={"rep": right}, device_id_type=MESH).wait_recv()
-
-    per_group = CHUNKS // GROUPS
+        lax.fori_loop(0, LIST // CHUNK, some, 0)
+        for copy in keep_copies(r, group, is_query):
+            copy.start()
+
+    def keep_copies(r, group, is_query):
+        rows = pl.ds(group * LIST, LIST)
+        if is_query:
+            return [pltpu.make_async_copy(staged_q.at[rows], qs.at[rows], keep_sem.at[2, group, 0])]
+        return [pltpu.make_async_copy(staged.at[a, r, rows], out.at[r, rows], keep_sem.at[a, group, r])
+                for a, out in enumerate((kall, vall))]
+
     table_copy = pltpu.make_async_copy(table_s, table_out, out_sem.at[0])
     destt_copy = pltpu.make_async_copy(destt_s, destt_out, out_sem.at[1])
     place_copy = pltpu.make_async_copy(place_s, place_out, out_sem.at[2])
-    for a, group in units:
-        if a == 0:
-            build(group)
-        wait_in(a, group)
-
-        def sort(i, _):
-            c = group * per_group + i
-            sorted_[a, rows_of(c)] = jnp.dot(
-                onehot[group, rows_of(i), :], rx[a, group], preferred_element_type=f32).astype(bf16)
-            if a < 2:
-                ycopy(a, 0, c).start()
-                ycopy(a, 1, c).start()
-            keep_copy(a, c).start()
+    pass_on(1, 0)
+    forward(0, 0)
+    tables()
+    table_copy.start()
+    destt_copy.start()
+    place_copy.start()
+    sort(rep, 0, False)
+    pass_on(0, 1)
+    forward(1, 0)
+    sort(left, 0, False)
+    sort(right, 0, False)
+    pass_on(1, 1)
+    forward(0, 1)
+    settle(0, 0)
+    settle(1, 0)
+    sort(far, 0, False)
+    sort(rep, 1, False)
+    forward(1, 1)
+    sort(left, 1, False)
+    sort(right, 1, False)
+    for group in range(GROUPS):
+        lax.fori_loop(1 - group, SLOTS, lambda slot, _: wait_slot(2, group, slot, _), 0)
+        if group == 0:
+            own_copy(2).wait()
+        sort(rep, group, True)
+    settle(0, 1)
+    settle(1, 1)
+    sort(far, 1, False)
+
+    table_copy.wait()
+    destt_copy.wait()
+    place_copy.wait()
+    for group in range(GROUPS):
+        for r in range(REPS):
+            for copy in keep_copies(r, group, False):
+                copy.wait()
+        keep_copies(rep, group, True)[0].wait()
+
+        def finish(c, _):
+            for a in range(2):
+                for kind in range(3):
+                    ycopy(a, kind, group, c).wait_send()
             return 0
 
-        lax.fori_loop(0, per_group, sort, 0)
-        if a == 0 and group == 0:
-            tables()
-            table_copy.start()
-            place_copy.start()
-            destt_copy.start()
-        if a < 2:
-            def forward(i, _):
-                c = group * per_group + i
-                wait_y(a, 0, c)
-                wait_y(a, 1, c)
-                ycopy(a, 2, c).start()
-                return 0
-
-            lax.fori_loop(0, per_group, forward, 0)
-
-    table_copy.wait()
-    place_copy.wait()
-    destt_copy.wait()
-
-    def finish(c, _):
+        lax.fori_loop(0, chunks, finish, 0)
         for a in range(3):
-            keep_copy(a, c).wait()
-        for a in range(2):
-            wait_y(a, 2, c)
-            for kind in range(3):
-                ycopy(a, kind, c).wait_send()
-        return 0
-
-    lax.fori_loop(0, CHUNKS, finish, 0)
-
-    for a in range(3):
-        for group in range(GROUPS):
             def sent(slot, _):
                 a2a_copy(a, group, slot).wait_send()
                 return 0
@@ -350,14 +394,15 @@
         in_specs=[any_, any_, any_, any_, vmem],
         out_specs=(any_,) * 6,
         scratch_shapes=[
-            pltpu.VMEM((3, GROUPS, LIST, DIM), bf16),
-            pltpu.VMEM((3, SPAN, DIM), bf16),
-            pltpu.VMEM((GROUPS, LIST, LIST), bf16),
+            pltpu.VMEM((2, REPS, GROUPS, LIST, DIM), bf16),
+            pltpu.VMEM((GROUPS, LIST, DIM), bf16),
+            pltpu.VMEM((2, REPS, SPAN, DIM), bf16),
+            pltpu.VMEM((SPAN, DIM), bf16),
             pltpu.VMEM((128, 128), i32),
-            pltpu.VMEM((128, 128), i32),
+            pltpu.VMEM((2, 128, 128), i32),
             pltpu.VMEM((128, 128), i32),
             pltpu.VMEM((4, 128, 128), f32),
-            pltpu.VMEM((HEADS, LOCAL), i32),
+            pltpu.VMEM((128, 128), i32),
             pltpu.VMEM((LOCAL, HEADS), i32),
             pltpu.VMEM((CLUSTERS, 128), i32),
             pltpu.VMEM((REPS + 1, CLUSTERS, 128), i32),
@@ -365,9 +410,9 @@
             pltpu.SemaphoreType.DMA((3, GROUPS, SLOTS)),
             pltpu.SemaphoreType.DMA((3,)),
             pltpu.SemaphoreType.DMA((128,)),
-            pltpu.SemaphoreType.DMA((2, 3, CHUNKS)),
-            pltpu.SemaphoreType.DMA((2, 3, CHUNKS)),
-            pltpu.SemaphoreType.DMA((3, CHUNKS)),
+            pltpu.SemaphoreType.DMA((2, 3, GROUPS, LIST // CHUNK)),
+            pltpu.SemaphoreType.DMA((2, 3, GROUPS, LIST // CHUNK)),
+            pltpu.SemaphoreType.DMA((3, GROUPS, REPS)),
             pltpu.SemaphoreType.DMA((3,)),
         ],
         compiler_params=pltpu.CompilerParams(

time: 154 us -> 151 us (0.981)
  Pallas kernels: 152 us -> 148 us
    pallas_call x1, Pallas kernels: 28.4 us -> 19.2 us  [attend_call(): pl.pallas_call(attend_kernel, out_shape=jax.ShapeDtypeStruct((SPAN, DIM),...]
    pallas_call x1, Pallas kernels: 23.5 us -> 32 us  [return_call(): pl.pallas_call(return_kernel, out_shape=jax.ShapeDtypeStruct((LOCAL, HALF...]
    pallas_call x1, Pallas kernels: 101 us -> 97 us  [gather_call(): pl.pallas_call(gather_kernel, out_shape=(jax.ShapeDtypeStruct((REPS, SPAN...]
where the time goes in v6:
time: 151 us; the launch traced here: 150 us
  Pallas kernels  148 us (98%)
  local copies, waits for them, and re-layouts  1.88 us (1%)
    pallas_call x1, Pallas kernels, gather_call(): pl.pallas_call(gather_kernel, out_shape=(jax.ShapeDtypeStruct((REPS, SPAN...  97 us
    pallas_call x1, Pallas kernels, return_call(): pl.pallas_call(return_kernel, out_shape=jax.ShapeDtypeStruct((LOCAL, HALF...  32 us
    pallas_call x1, Pallas kernels, attend_call(): pl.pallas_call(attend_kernel, out_shape=jax.ShapeDtypeStruct((SPAN, DIM),...  19.2 us

profile of v6, /device:TPU:6, one launch (start us, length us, event | category | flops | bytes accessed | tf_op | source)
XLA Modules:
  0.0 150.1 jit_solution(6899999345640416745)
XLA Ops:
  0.0 97.0 %gather_sorted.1 = (bf16[4,4096,128]{2,1,0:T(8,128)(2,1)}, bf16[4,4096,128]{2,1,0:T(8,128)(2,1)}, bf16[4096,128]{1,0:T(8,128)(2,1)}, s32[64,128]{1,0:T(8,128)}, ...) custom-call(bf16[128,4096]{1,0:T(8,128)(2,1)} %bitcast.8, bf16[128,4096]{1,0:T(8,128)(2,1)} %bitcast.9, ...), custom_call_target="tpu_custom_call" | custom-call | tf_op jit(solution)/shard_map/gather_sorted/pallas_call | solution.py:384
  97.0 19.2 %attend.1.mixed_in = bf16[4096,128]{1,0:T(8,128)(2,1)} custom-call(s32[64,128]{1,0:T(8,128)} %get-tuple-element.11.table, s32[8,64]{1,0:T(8,128)} %bitcast.11, s32[64]{0:T(128)} %bitcast.12, s32[1]{0:T(128)} %bitcast.6.rep_ref, s32[5,64,128]{2,1,0:T(8,128)} %get-tuple-element.12.place_ref, bf16[4,4096,128]{2,1,0:T(8,128)(2,1)} %get-tuple-element.13.kall, ...), custom_call_target="tpu_custom_call" | custom-call | tf_op jit(solution)/shard_map/attend/pallas_call | solution.py:582
  116.2 32.0 %return_tokens.1 = bf16[128,2048]{1,0:T(8,128)(2,1)} custom-call(bf16[4096,128]{1,0:T(8,128)(2,1)} %attend.1.mixed_in, s32[128,32]{1,0:T(8,128)} %get-tuple-element.16.destt_in), custom_call_target="tpu_custom_call" | custom-call | tf_op jit(solution)/shard_map/return_tokens/pallas_call | solution.py:713
  148.2 1.9 %copy.8 = bf16[128,2048]{1,0:T(8,128)(2,1)} copy(bf16[128,2048]{1,0:T(8,128)(2,1)} %return_tokens.1) | data formatting | bytes 1048576
